TPU v7x, 256 devices: a whole 4x4x8 slice. The times are simulated.
256 devices in a mesh: seq: 64 (over y, x_hi, z), grp: 4 (over x_lo, core).
Axes of the slice: x: 4 (x_hi: 2, x_lo: 2; x = x_hi * 2 + x_lo), y: 4, z: 8, core: 2. Of those that a mesh axis runs over, the one named last changes fastest.
Arguments:
- query_gate: bfloat16 [4, 8192, 2048], P('grp', 'seq'), may hold values from -6 to 6
- key_gate: bfloat16 [4, 8192, 2048], P('grp', 'seq'), may hold values from -6 to 6
- value_in: bfloat16 [4, 8192, 2048], P('grp', 'seq'), may hold values from -6 to 6
- grad_out: bfloat16 [4, 8192, 2048], P('grp', 'seq'), may hold values from -6 to 6
- filter_taps: float32 [8192, 2048], P('seq'), may hold values from -6 to 6
- skip_gain: float32 [2048], replicated, may hold values from 0.25 to 2
Outputs:
- query_grad: bfloat16 [4, 8192, 2048], P('grp', 'seq')
- key_grad: bfloat16 [4, 8192, 2048], P('grp', 'seq')
- value_grad: bfloat16 [4, 8192, 2048], P('grp', 'seq')
- filter_grad: float32 [8192, 2048], P('seq')
All inputs are finite; a program needn't handle non-finite values.
Results may differ from a plain program's by a relative error of at most 0.001.
Values sent between devices are 32-bit elements; how exact they have to be, the bound alone decides.
No kernel may reach another device: no remote copies, remote signals or barrier semaphores. Data moves between devices by JAX's collectives and lax.ppermute only.
A program may use at most 128 MiB of HBM per device.

v0:
```python
import math

import jax
import jax.numpy as jnp
import numpy as np
from jax import lax
from jax.sharding import PartitionSpec as P

highest = lax.Precision.HIGHEST


def angle_table(row_index, col_index, period):
    turns = row_index[:, None] * col_index[None, :] % period
    phase = turns.astype(jnp.float32) * (2.0 * math.pi / period)
    return (jnp.cos(phase), jnp.sin(phase))


def along_rows(table, blocks):
    return jnp.einsum("kn,jnw->jkw", table, blocks, precision=highest)


def class_order(seq_parts):
    listed = [0, seq_parts]
    for member in range(1, seq_parts):
        listed = listed + [member, 2 * seq_parts - member]
    return jnp.asarray(np.array(listed, dtype=np.int32))


def forward_transform(signal, imag_start, order):
    seq_parts = lax.axis_size("seq")
    seq_index = lax.axis_index("seq")
    rows_dev, col_width = signal.shape
    sub_rows = rows_dev // seq_parts
    full_len = 2 * seq_parts * rows_dev
    pieces = signal.reshape(seq_parts, sub_rows * col_width)
    arrived = lax.all_to_all(pieces, "seq", split_axis=0, concat_axis=0, tiled=True)
    cos_first, sin_first = angle_table(order, jnp.arange(seq_parts, dtype=jnp.int32), 2 * seq_parts)
    cos_part = jnp.dot(cos_first, arrived, precision=highest).reshape(
        2 * seq_parts, sub_rows, col_width
    )
    sin_part = jnp.dot(sin_first, arrived, precision=highest).reshape(
        2 * seq_parts, sub_rows, col_width
    )
    first_real = cos_part[:, :, :imag_start] + sin_part[:, :, imag_start:]
    first_imag = cos_part[:, :, imag_start:] - sin_part[:, :, :imag_start]
    offsets = seq_index * sub_rows + jnp.arange(sub_rows, dtype=jnp.int32)
    twist_cos, twist_sin = angle_table(order, offsets, full_len)
    twist_cos = twist_cos[:, :, None]
    twist_sin = twist_sin[:, :, None]
    turned_real = first_real * twist_cos + first_imag * twist_sin
    turned_imag = first_imag * twist_cos - first_real * twist_sin
    middle_real, middle_imag = (
        lax.all_to_all(turned_real, "seq", split_axis=0, concat_axis=1, tiled=True),
        lax.all_to_all(turned_imag, "seq", split_axis=0, concat_axis=1, tiled=True),
    )
    cos_last, sin_last = angle_table(
        jnp.arange(rows_dev, dtype=jnp.int32), jnp.arange(rows_dev, dtype=jnp.int32), rows_dev
    )
    spec_real = along_rows(cos_last, middle_real) + along_rows(sin_last, middle_imag)
    spec_imag = along_rows(cos_last, middle_imag) - along_rows(sin_last, middle_real)
    return (spec_real, spec_imag)


def inverse_transform(spec_real, spec_imag, order):
    seq_parts = lax.axis_size("seq")
    seq_index = lax.axis_index("seq")
    rows_dev = spec_real.shape[1]
    col_width = spec_real.shape[2]
    sub_rows = rows_dev // seq_parts
    full_len = 2 * seq_parts * rows_dev
    cos_last, sin_last = angle_table(
        jnp.arange(rows_dev, dtype=jnp.int32), jnp.arange(rows_dev, dtype=jnp.int32), rows_dev
    )
    back_real = along_rows(cos_last, spec_real) - along_rows(sin_last, spec_imag)
    back_imag = along_rows(cos_last, spec_imag) + along_rows(sin_last, spec_real)
    pair_index = lax.dynamic_slice_in_dim(order, 2 * seq_index, 2, 0)
    twist_cos, twist_sin = angle_table(pair_index, jnp.arange(rows_dev, dtype=jnp.int32), full_len)
    twist_cos = twist_cos[:, :, None]
    twist_sin = twist_sin[:, :, None]
    turned_real = back_real * twist_cos - back_imag * twist_sin
    turned_imag = back_imag * twist_cos + back_real * twist_sin
    mixed_real, mixed_imag = (
        lax.all_to_all(turned_real, "seq", split_axis=1, concat_axis=0, tiled=True),
        lax.all_to_all(turned_imag, "seq", split_axis=1, concat_axis=0, tiled=True),
    )
    flat_real = mixed_real.reshape(2 * seq_parts, sub_rows * col_width)
    flat_imag = mixed_imag.reshape(2 * seq_parts, sub_rows * col_width)
    cos_first, sin_first = angle_table(jnp.arange(seq_parts, dtype=jnp.int32), order, 2 * seq_parts)
    out_real = (
        jnp.dot(cos_first, flat_real, precision=highest)
        - jnp.dot(sin_first, flat_imag, precision=highest)
    ) / full_len
    out_imag = (
        jnp.dot(cos_first, flat_imag, precision=highest)
        + jnp.dot(sin_first, flat_real, precision=highest)
    ) / full_len
    ret_real, ret_imag = (
        lax.all_to_all(out_real, "seq", split_axis=0, concat_axis=1, tiled=True),
        lax.all_to_all(out_imag, "seq", split_axis=0, concat_axis=1, tiled=True),
    )
    return (ret_real.reshape(rows_dev, col_width), ret_imag.reshape(rows_dev, col_width))


def split_mirror(zed_real, zed_imag, seq_index):
    flip_real = zed_real[:, ::-1]
    flip_imag = zed_imag[:, ::-1]
    at_anchor = seq_index == 0
    neg_real = jnp.where(
        at_anchor, jnp.stack([jnp.roll(flip_real[0], 1, axis=0), flip_real[1]]), flip_real[::-1]
    )
    neg_imag = jnp.where(
        at_anchor, jnp.stack([jnp.roll(flip_imag[0], 1, axis=0), flip_imag[1]]), flip_imag[::-1]
    )
    first_real = 0.5 * (zed_real + neg_real)
    first_imag = 0.5 * (zed_imag - neg_imag)
    second_real = 0.5 * (zed_imag + neg_imag)
    second_imag = -0.5 * (zed_real - neg_real)
    return (first_real, first_imag, second_real, second_imag)


def body(query_gate, key_gate, value_in, grad_out, filter_taps, skip_gain):
    query_rows = query_gate[0].astype(jnp.float32)
    key_rows = key_gate[0].astype(jnp.float32)
    value_rows = value_in[0].astype(jnp.float32)
    grad_rows = grad_out[0].astype(jnp.float32)
    rows_dev, channels = filter_taps.shape
    seq_parts = lax.axis_size("seq")
    scale = 1.0 / math.sqrt(seq_parts * rows_dev)
    product = key_rows * value_rows
    gated_grad = query_rows * grad_rows
    share = channels // lax.axis_size("grp")
    own_taps = lax.dynamic_slice_in_dim(filter_taps, lax.axis_index("grp") * share, share, 1)
    order = class_order(seq_parts)
    halfway = own_taps.shape[1] // 2
    signal = jnp.concatenate(
        [product, own_taps[:, :halfway], gated_grad, own_taps[:, halfway:]], axis=1
    )
    zed_real, zed_imag = forward_transform(signal, channels + halfway, order)
    first_real, first_imag, second_real, second_imag = split_mirror(
        zed_real, zed_imag, lax.axis_index("seq")
    )
    prod_real = first_real[:, :, :channels]
    prod_imag = first_imag[:, :, :channels]
    grad_real = second_real[:, :, :channels]
    grad_imag = second_imag[:, :, :channels]
    own_real = jnp.concatenate([first_real[:, :, channels:], second_real[:, :, channels:]], axis=2)
    own_imag = jnp.concatenate([first_imag[:, :, channels:], second_imag[:, :, channels:]], axis=2)
    filt_real, filt_imag = (
        lax.all_gather(own_real, "grp", axis=2, tiled=True),
        lax.all_gather(own_imag, "grp", axis=2, tiled=True),
    )
    conv_real = prod_real * filt_real - prod_imag * filt_imag
    conv_imag = prod_real * filt_imag + prod_imag * filt_real
    back_real = grad_real * filt_real + grad_imag * filt_imag
    back_imag = grad_imag * filt_real - grad_real * filt_imag
    tap_real = grad_real * prod_real + grad_imag * prod_imag
    tap_imag = grad_imag * prod_real - grad_real * prod_imag
    tap_real, tap_imag = (
        lax.psum_scatter(tap_real, "grp", scatter_dimension=2, tiled=True),
        lax.psum_scatter(tap_imag, "grp", scatter_dimension=2, tiled=True),
    )
    half = tap_real.shape[2] // 2
    packed_real = jnp.concatenate(
        [conv_real - back_imag, tap_real[:, :, :half] - tap_imag[:, :, half:]], axis=2
    )
    packed_imag = jnp.concatenate(
        [conv_imag + back_real, tap_imag[:, :, :half] + tap_real[:, :, half:]], axis=2
    )
    out_real, out_imag = inverse_transform(packed_real, packed_imag, order)
    conv_out = out_real[:, :channels]
    back_conv = out_imag[:, :channels]
    tap_part = jnp.concatenate([out_real[:, channels:], out_imag[:, channels:]], axis=1)
    tap_total = lax.all_gather(tap_part, "grp", axis=1, tiled=True)
    mixed = scale * conv_out + skip_gain * product
    product_grad = scale * back_conv + skip_gain * gated_grad
    query_grad = (grad_rows * mixed).astype(jnp.bfloat16)[None]
    key_grad = (product_grad * value_rows).astype(jnp.bfloat16)[None]
    value_grad = (product_grad * key_rows).astype(jnp.bfloat16)[None]
    filter_grad = scale * tap_total
    return (query_grad, key_grad, value_grad, filter_grad)


def solution(mesh):
    placed = (
        P("grp", "seq", None),
        P("grp", "seq", None),
        P("grp", "seq", None),
        P("grp", "seq", None),
        P("seq", None),
        P(),
    )
    return jax.shard_map(
        body,
        mesh=mesh,
        in_specs=placed,
        out_specs=(
            P("grp", "seq", None),
            P("grp", "seq", None),
            P("grp", "seq", None),
            P("seq", None),
        ),
        check_vma=False,
    )
```

profile of v0, /device:TPU:1, one launch (start us, length us, event | category | flops | bytes accessed | tf_op | source)
XLA Modules:
  0.0 729.3 jit_solution(6153750217225060391)
XLA Ops:
  14.1 15.8 %all-to-all-start = ((f32[64,1,9216]{2,1,0:T(1,128)}), f32[64,1,9216]{2,1,0:T(1,128)S(1)}, u32[]{:S(2)}, u32[]{:S(2)}) async-start(f32[64,1,9216]{2,1,0:T(1,128)} %all_to_all.76), calls=%async_computation | async-start | bytes 4718592 | tf_op jit(solution)/shard_map/all_to_all | solution.py:36
  30.0 54.0 %all-to-all-done = f32[64,1,9216]{2,1,0:T(1,128)S(1)} async-done(((f32[64,1,9216]{2,1,0:T(1,128)}), f32[64,1,9216]{2,1,0:T(1,128)S(1)}, u32[]{:S(2)}, u32[]{:S(2)}) %all-to-all-start) | async-done | bytes 2359328 | tf_op jit(solution)/shard_map/all_to_all | solution.py:36
  97.9 9.5 %all-to-all-start.2 = ((f32[128,2,2304]{2,1,0:T(2,128)}), f32[128,2,2304]{2,1,0:T(2,128)S(1)}, u32[]{:S(2)}, u32[]{:S(2)}) async-start(f32[128,2,2304]{2,1,0:T(2,128)} %copy.33), calls=%async_computation.2 | async-start | bytes 4718592 | tf_op jit(solution)/shard_map/all_to_all | solution.py:54
  112.4 48.6 %all-to-all-done.2 = f32[128,2,2304]{2,1,0:T(2,128)S(1)} async-done(((f32[128,2,2304]{2,1,0:T(2,128)}), f32[128,2,2304]{2,1,0:T(2,128)S(1)}, u32[]{:S(2)}, u32[]{:S(2)}) %all-to-all-start.2) | async-done | bytes 2359328 | tf_op jit(solution)/shard_map/all_to_all | solution.py:54
  161.0 10.3 %all-to-all-start.1 = ((f32[128,2,2304]{2,1,0:T(2,128)}), f32[128,2,2304]{2,1,0:T(2,128)}, u32[]{:S(2)}, u32[]{:S(2)}) async-start(f32[128,2,2304]{2,1,0:T(2,128)} %copy.31), calls=%async_computation.1 | async-start | bytes 4718592 | tf_op jit(solution)/shard_map/all_to_all | solution.py:53
  179.9 44.8 %all-to-all-done.1 = f32[128,2,2304]{2,1,0:T(2,128)} async-done(((f32[128,2,2304]{2,1,0:T(2,128)}), f32[128,2,2304]{2,1,0:T(2,128)}, u32[]{:S(2)}, u32[]{:S(2)}) %all-to-all-start.1) | async-done | bytes 2359328 | tf_op jit(solution)/shard_map/all_to_all | solution.py:53
  235.9 11.8 %rev.9 = f32[2,128,2304]{2,1,0:T(8,128)} reverse(f32[2,128,2304]{2,1,0:T(8,128)S(1)} %fusion.5), dimensions={0,1} | reverse | bytes 4718592 | tf_op jit(solution)/shard_map/rev | solution.py:112
  255.6 11.8 %rev.8 = f32[2,128,2304]{2,1,0:T(8,128)} reverse(f32[2,128,2304]{2,1,0:T(8,128)S(1)} %fusion.4), dimensions={0,1} | reverse | bytes 4718592 | tf_op jit(solution)/shard_map/rev | solution.py:109
  267.5 10.0 %slice.138 = f32[1,127,2304]{2,1,0:T(8,128)} reverse(f32[1,127,2304]{2,1,0:T(8,128)} %slice.166), dimensions={1} | reverse | bytes 2340864 | tf_op jit(solution)/shard_map/jit(_roll_static)/slice | solution.py:112
  291.0 6.0 slice.129
  313.7 29.1 %all-gather.4.cloned.1.call-done = f32[2,128,2048]{2,1,0:T(8,128)} async-done(((f32[2,128,512]{2,1,0:T(8,128)}), f32[2,128,2048]{2,1,0:T(8,128)}) %all-gather.4.cloned.1.call-update) | async-done | bytes 2097168 | tf_op jit(solution)/shard_map/all_gather | solution.py:149
  342.8 35.0 %all-gather.6.cloned.1.call-done = f32[2,128,2048]{2,1,0:T(8,128)} async-done(((f32[2,128,512]{2,1,0:T(8,128)}), f32[2,128,2048]{2,1,0:T(8,128)}) %all-gather.6.cloned.1.call-update) | async-done | bytes 2097168 | tf_op jit(solution)/shard_map/all_gather | solution.py:150
  377.7 7.6 %subtract_subtract_fusion = (f32[2,128,2048]{2,1,0:T(8,128)}, f32[2,128,2048]{2,1,0:T(8,128)S(1)}, f32[2,128,2048]{2,1,0:T(8,128)}, f32[2,128,2048]{2,1,0:T(8,128)}) fusion(f32[2,128,2048]{2,1,0:T(8,128)} %all-gather.6.cloned.1.call-done, f32[2,128,2048]{2,1,0:T(8,128)} %all-gather.4.cloned.1.call-done, f32[2,128,2304]{2,1,0:T(8,128)} %copy-done.9, ...), kind=kLoop, calls=%fused_computation.38 | loop fusion | flops 10485760 | bytes 20971520 | tf_op jit(solution)/shard_map/sub | solution.py:164
  386.1 30.9 %reduce-scatter.3.cloned.1.call-done = f32[2,128,512]{2,1,0:T(8,128)} async-done(((f32[2,128,2048]{2,1,0:T(8,128)}), f32[2,128,512]{2,1,0:T(8,128)}) %reduce-scatter.3.cloned.1.call-update) | async-done | bytes 524304 | tf_op jit(solution)/shard_map/reduce_scatter | solution.py:159
  417.0 34.3 %reduce-scatter.5.cloned.1.call-done = f32[2,128,512]{2,1,0:T(8,128)} async-done(((f32[2,128,2048]{2,1,0:T(8,128)}), f32[2,128,512]{2,1,0:T(8,128)}) %reduce-scatter.5.cloned.1.call-update) | async-done | bytes 524304 | tf_op jit(solution)/shard_map/reduce_scatter | solution.py:160
  477.4 12.3 %all-to-all-start.3 = ((f32[2,128,2304]{2,0,1:T(2,128)}), f32[2,128,2304]{2,0,1:T(2,128)S(1)}, u32[]{:S(2)}, u32[]{:S(2)}) async-start(f32[2,128,2304]{2,0,1:T(2,128)} %copy.39), calls=%async_computation.5 | async-start | bytes 4718592 | tf_op jit(solution)/shard_map/all_to_all | solution.py:83
  494.7 49.8 %all-to-all-done.3 = f32[2,128,2304]{2,0,1:T(2,128)S(1)} async-done(((f32[2,128,2304]{2,0,1:T(2,128)}), f32[2,128,2304]{2,0,1:T(2,128)S(1)}, u32[]{:S(2)}, u32[]{:S(2)}) %all-to-all-start.3) | async-done | bytes 2359328 | tf_op jit(solution)/shard_map/all_to_all | solution.py:83
  544.5 9.6 %all-to-all-start.4 = ((f32[2,128,2304]{2,0,1:T(2,128)}), f32[2,128,2304]{2,0,1:T(2,128)}, u32[]{:S(2)}, u32[]{:S(2)}) async-start(f32[2,128,2304]{2,0,1:T(2,128)} %copy.41), calls=%async_computation.6 | async-start | bytes 4718592 | tf_op jit(solution)/shard_map/all_to_all | solution.py:84
  556.9 51.2 %all-to-all-done.4 = f32[2,128,2304]{2,0,1:T(2,128)} async-done(((f32[2,128,2304]{2,0,1:T(2,128)}), f32[2,128,2304]{2,0,1:T(2,128)}, u32[]{:S(2)}, u32[]{:S(2)}) %all-to-all-start.4) | async-done | bytes 2359328 | tf_op jit(solution)/shard_map/all_to_all | solution.py:84
  616.3 9.7 %all-to-all-start.5 = ((f32[64,1,4608]{2,1,0:T(1,128)}), f32[64,1,4608]{2,1,0:T(1,128)S(1)}, u32[]{:S(2)}, u32[]{:S(2)}) async-start(f32[64,1,4608]{2,1,0:T(1,128)} %copy.43), calls=%async_computation.7 | async-start | bytes 2359296 | tf_op jit(solution)/shard_map/all_to_all | solution.py:98
  633.0 22.0 %all-to-all-done.5 = f32[64,1,4608]{2,1,0:T(1,128)S(1)} async-done(((f32[64,1,4608]{2,1,0:T(1,128)}), f32[64,1,4608]{2,1,0:T(1,128)S(1)}, u32[]{:S(2)}, u32[]{:S(2)}) %all-to-all-start.5) | async-done | bytes 1179680 | tf_op jit(solution)/shard_map/all_to_all | solution.py:98
  655.0 8.6 %all-to-all-start.6 = ((f32[64,1,4608]{2,1,0:T(1,128)}), f32[64,1,4608]{2,1,0:T(1,128)S(1)}, u32[]{:S(2)}, u32[]{:S(2)}) async-start(f32[64,1,4608]{2,1,0:T(1,128)} %copy.44), calls=%async_computation.8 | async-start | bytes 2359296 | tf_op jit(solution)/shard_map/all_to_all | solution.py:99
  667.6 23.8 %all-to-all-done.6 = f32[64,1,4608]{2,1,0:T(1,128)S(1)} async-done(((f32[64,1,4608]{2,1,0:T(1,128)}), f32[64,1,4608]{2,1,0:T(1,128)S(1)}, u32[]{:S(2)}, u32[]{:S(2)}) %all-to-all-start.6) | async-done | bytes 1179680 | tf_op jit(solution)/shard_map/all_to_all | solution.py:99
  699.3 20.8 %all-gather.8.cloned.1.call-done = f32[128,2048]{1,0:T(8,128)} async-done(((f32[128,512]{1,0:T(8,128)}), f32[128,2048]{1,0:T(8,128)}) %all-gather.8.cloned.1.call-update) | async-done | bytes 1048592 | tf_op jit(solution)/shard_map/all_gather | solution.py:173
  (112 shorter events, 147.6 us)
Async XLA Ops:
  14.1 15.8 %copy-start.15 = (s32[128]{0:T(128)S(1)}, s32[128]{0:T(128)}, u32[]{:S(2)}) copy-start(s32[128]{0:T(128)} %constant.91.clone) | copy-start | bytes 1540
  14.1 69.9 %all-to-all-start = ((f32[64,1,9216]{2,1,0:T(1,128)}), f32[64,1,9216]{2,1,0:T(1,128)S(1)}, u32[]{:S(2)}, u32[]{:S(2)}) async-start(f32[64,1,9216]{2,1,0:T(1,128)} %all_to_all.76), calls=%async_computation | async-start | bytes 4718592 | tf_op jit(solution)/shard_map/all_to_all | solution.py:36
  97.9 63.1 %all-to-all-start.2 = ((f32[128,2,2304]{2,1,0:T(2,128)}), f32[128,2,2304]{2,1,0:T(2,128)S(1)}, u32[]{:S(2)}, u32[]{:S(2)}) async-start(f32[128,2,2304]{2,1,0:T(2,128)} %copy.33), calls=%async_computation.2 | async-start | bytes 4718592 | tf_op jit(solution)/shard_map/all_to_all | solution.py:54
  161.0 63.7 %all-to-all-start.1 = ((f32[128,2,2304]{2,1,0:T(2,128)}), f32[128,2,2304]{2,1,0:T(2,128)}, u32[]{:S(2)}, u32[]{:S(2)}) async-start(f32[128,2,2304]{2,1,0:T(2,128)} %copy.31), calls=%async_computation.1 | async-start | bytes 4718592 | tf_op jit(solution)/shard_map/all_to_all | solution.py:53
  171.3 171.5 %all-gather.4.cloned.1.call-start = ((), (), s32[]{:S(2)}) async-start(), calls=%async_computation.9 | async-start | bytes 2621440 | tf_op jit(solution)/shard_map/all_gather | solution.py:149
  176.0 3.9 copy-start.4
  234.1 13.7 %copy-start.2 = (f32[2,128,2304]{2,1,0:T(8,128)}, f32[2,128,2304]{2,1,0:T(8,128)S(1)}, u32[]{:S(2)}) copy-start(f32[2,128,2304]{2,1,0:T(8,128)S(1)} %fusion.5) | copy-start | bytes 7077892
  254.4 13.0 %copy-start = (f32[2,128,2304]{2,1,0:T(8,128)}, f32[2,128,2304]{2,1,0:T(8,128)S(1)}, u32[]{:S(2)}) copy-start(f32[2,128,2304]{2,1,0:T(8,128)S(1)} %fusion.4) | copy-start | bytes 7077892
  267.5 10.0 %slice-start.1 = ((f32[2,128,2304]{2,1,0:T(8,128)}), f32[1,128,2304]{2,1,0:T(8,128)S(1)}, s32[]{:S(2)}) async-start(f32[2,128,2304]{2,1,0:T(8,128)} %copy-done.2), calls=%async_computation.15 | async-start | bytes 2359296 | tf_op jit(solution)/shard_map/slice | solution.py:112
  277.4 7.4 %copy-start.3 = (f32[2,128,2304]{2,1,0:T(8,128)S(1)}, f32[2,128,2304]{2,1,0:T(8,128)}, u32[]{:S(2)}) copy-start(f32[2,128,2304]{2,1,0:T(8,128)} %copy-done.2) | copy-start | bytes 7077892
  285.4 5.6 copy-start.13
  288.8 8.1 %slice-start = ((f32[2,128,2304]{2,1,0:T(8,128)}), f32[1,128,2304]{2,1,0:T(8,128)S(1)}, s32[]{:S(2)}) async-start(f32[2,128,2304]{2,1,0:T(8,128)} %copy-done), calls=%async_computation.14 | async-start | bytes 2359296 | tf_op jit(solution)/shard_map/slice | solution.py:109
  297.0 7.4 %copy-start.1 = (f32[2,128,2304]{2,1,0:T(8,128)S(1)}, f32[2,128,2304]{2,1,0:T(8,128)}, u32[]{:S(2)}) copy-start(f32[2,128,2304]{2,1,0:T(8,128)} %copy-done) | copy-start | bytes 7077892
  304.9 4.9 copy-start.14
  310.7 67.0 %all-gather.6.cloned.1.call-start = ((), (), s32[]{:S(2)}) async-start(), calls=%async_computation.10 | async-start | bytes 2621440 | tf_op jit(solution)/shard_map/all_gather | solution.py:150
  313.6 103.4 %reduce-scatter.3.cloned.1.call-start = ((), (), s32[]{:S(2)}) async-start(), calls=%async_computation.11 | async-start | bytes 2621440 | tf_op jit(solution)/shard_map/reduce_scatter | solution.py:159
  385.3 66.0 %reduce-scatter.5.cloned.1.call-start = ((), (), s32[]{:S(2)}) async-start(), calls=%async_computation.12 | async-start | bytes 2621440 | tf_op jit(solution)/shard_map/reduce_scatter | solution.py:160
  458.1 4.1 copy-start.8
  477.4 67.1 %all-to-all-start.3 = ((f32[2,128,2304]{2,0,1:T(2,128)}), f32[2,128,2304]{2,0,1:T(2,128)S(1)}, u32[]{:S(2)}, u32[]{:S(2)}) async-start(f32[2,128,2304]{2,0,1:T(2,128)} %copy.39), calls=%async_computation.5 | async-start | bytes 4718592 | tf_op jit(solution)/shard_map/all_to_all | solution.py:83
  544.5 63.6 %all-to-all-start.4 = ((f32[2,128,2304]{2,0,1:T(2,128)}), f32[2,128,2304]{2,0,1:T(2,128)}, u32[]{:S(2)}, u32[]{:S(2)}) async-start(f32[2,128,2304]{2,0,1:T(2,128)} %copy.41), calls=%async_computation.6 | async-start | bytes 4718592 | tf_op jit(solution)/shard_map/all_to_all | solution.py:84
  616.3 38.7 %all-to-all-start.5 = ((f32[64,1,4608]{2,1,0:T(1,128)}), f32[64,1,4608]{2,1,0:T(1,128)S(1)}, u32[]{:S(2)}, u32[]{:S(2)}) async-start(f32[64,1,4608]{2,1,0:T(1,128)} %copy.43), calls=%async_computation.7 | async-start | bytes 2359296 | tf_op jit(solution)/shard_map/all_to_all | solution.py:98
  655.0 36.4 %all-to-all-start.6 = ((f32[64,1,4608]{2,1,0:T(1,128)}), f32[64,1,4608]{2,1,0:T(1,128)S(1)}, u32[]{:S(2)}, u32[]{:S(2)}) async-start(f32[64,1,4608]{2,1,0:T(1,128)} %copy.44), calls=%async_computation.8 | async-start | bytes 2359296 | tf_op jit(solution)/shard_map/all_to_all | solution.py:99
  663.6 56.6 %all-gather.8.cloned.1.call-start = ((), (), s32[]{:S(2)}) async-start(), calls=%async_computation.13 | async-start | bytes 1310720 | tf_op jit(solution)/shard_map/all_gather | solution.py:173
  667.5 28.5 %copy-start.16 = (f32[2048]{0:T(1024)S(1)}, f32[2048]{0:T(1024)}, u32[]{:S(2)}) copy-start(f32[2048]{0:T(1024)} %param.12) | copy-start | bytes 24580
  (7 other events, 12.5 us)
Sparse Core Ops, SparseCore 0:
  310.9 31.8 all-gather.3
  345.2 32.5 all-gather.5
  385.5 31.4 reduce-scatter.2
  419.6 31.7 reduce-scatter.4
  696.2 23.9 all-gather.7
where the time goes:
time: 734 us; the launch traced here: 729 us
  waiting for transfers between devices  444 us (60%)
  local copies, waits for them, and re-layouts  107 us (15%)
  starting transfers between devices  76.6 us (10%)
  matrix products  49.2 us (7%)
  other arithmetic  37.8 us (5%)
  between operations  14.5 us (2%)
    all_to_all x1, waiting for transfers between devices, forward_transform(): lax.all_to_all(pieces, 'seq', split_axis=0, concat_axis=0, tiled=True)  54 us
    all_to_all x1, waiting for transfers between devices, inverse_transform(): lax.all_to_all(turned_imag, 'seq', split_axis=1, concat_axis=0, tiled=True)  51.2 us
    all_to_all x1, waiting for transfers between devices, inverse_transform(): lax.all_to_all(turned_real, 'seq', split_axis=1, concat_axis=0, tiled=True)  49.8 us
    all_to_all x1, waiting for transfers between devices, forward_transform(): lax.all_to_all(turned_imag, 'seq', split_axis=0, concat_axis=1, tiled=True)  48.6 us
    all_to_all x1, waiting for transfers between devices, forward_transform(): lax.all_to_all(turned_real, 'seq', split_axis=0, concat_axis=1, tiled=True)  44.8 us
    all_gather x1, waiting for transfers between devices, body(): lax.all_gather(own_imag, 'grp', axis=2, tiled=True)  35 us
    reduce_scatter x1, waiting for transfers between devices, body(): lax.psum_scatter(tap_imag, 'grp', scatter_dimension=2, tiled=True)  34.3 us
    dot_general x8, matrix products, along_rows(): return jnp.einsum('kn,jnw->jkw', table, blocks, precision=highest)  33.4 us
  transfers between devices with their start and end apart: 12, of which 12 were waited for; matrix products, arithmetic and copies ran while one was open for 5% of the time, Pallas kernels for 0%

commit v1 on v0

v1 whole, which is shorter than its diff:
```python
import functools
import math

import jax
import jax.numpy as jnp
import numpy as np
from jax import lax
from jax.experimental import pallas as pl
from jax.experimental.pallas import tpu as pltpu
from jax.sharding import PartitionSpec as P

f32 = jnp.float32
bf16 = jnp.bfloat16


def halves(table):
    high = np.asarray(table, np.float32).astype(jnp.bfloat16)
    low = (table - high.astype(np.float64)).astype(np.float32).astype(jnp.bfloat16)
    return high, low


def transform_tables(blocks, rows, scale):
    full = 2 * blocks * rows
    k1 = np.arange(blocks)[:, None] + 0.5
    first = 2.0 * math.pi * k1 * np.arange(blocks)[None, :] / (2 * blocks)
    twist = 2.0 * math.pi * k1 * np.arange(rows)[None, :] / full
    last = 2.0 * math.pi * np.arange(rows)[:, None] * np.arange(rows)[None, :] / rows
    c1, s1 = np.cos(first), np.sin(first)
    c2, s2 = np.cos(last), np.sin(last)
    ahead1 = halves(np.concatenate([c1, -s1], axis=0))
    ahead2 = halves(np.block([[c2, -s2], [s2, c2]]))
    back2 = halves(np.block([[c2, s2], [-s2, c2]]))
    back1 = halves(np.concatenate([c1.T, -s1.T], axis=1) * (2.0 * scale / full))
    stack1 = np.concatenate([ahead1[0], ahead1[1], ahead1[0]], axis=1)
    unstack1 = np.concatenate([back1[0], back1[1], back1[0]], axis=1)
    turn = np.stack([np.cos(twist), np.sin(twist)]).astype(np.float32)
    return stack1, turn, np.stack(ahead2), np.stack(back2), unstack1


def split(value):
    high = value.astype(bf16)
    return high, (value - high.astype(f32)).astype(bf16)


def dot(left, right):
    return jnp.dot(left, right, preferred_element_type=f32)


def dot3(value, table_ref):
    high, low = split(value)
    return dot(high, table_ref[0]) + dot(low, table_ref[0]) + dot(high, table_ref[1])


def pack_kernel(slots, query_ref, key_ref, value_ref, grad_ref, taps_ref, out_ref):
    rows, channels = query_ref.shape
    devices = channels // slots
    share = taps_ref.shape[1] // devices
    piece = 2 * slots + share
    per = devices // rows
    for block in range(channels // rows):
        slot, start = block // per, block % per * rows * piece
        cols = pl.ds(block * rows, rows)
        product = key_ref[:, cols].astype(f32) * value_ref[:, cols].astype(f32)
        gated = query_ref[:, cols].astype(f32) * grad_ref[:, cols].astype(f32)
        out_ref[pl.ds(start + slot, rows, stride=piece), :] = product.T
        out_ref[pl.ds(start + slots + slot, rows, stride=piece), :] = gated.T
    for block in range(share * per):
        slot, start = block // per, block % per * rows * piece
        taps = taps_ref[:, pl.ds(block * rows, rows)]
        out_ref[pl.ds(start + 2 * slots + slot, rows, stride=piece), :] = taps.T


def spectral_kernel(
    slots, groups, blocks, data_ref, first_ref, turn_ref, ahead_ref, back_ref, last_ref, out_ref
):
    share = slots // groups
    piece = 2 * slots + share
    rows = data_ref.shape[1]
    cos_t, sin_t = turn_ref[0], turn_ref[1]

    def rows_of(start):
        return pl.ds(start, blocks, stride=groups * piece)

    def forward(signals):
        high, low = split(jnp.concatenate(signals, axis=1))
        freq = dot(first_ref[...], jnp.concatenate([high, high, low], axis=0))
        turned = []
        for i in range(len(signals)):
            real = freq[:blocks, i * rows : (i + 1) * rows]
            imag = freq[blocks:, i * rows : (i + 1) * rows]
            turned.append(
                jnp.concatenate(
                    [real * cos_t + imag * sin_t, imag * cos_t - real * sin_t], axis=1
                )
            )
        spec = dot3(jnp.concatenate(turned, axis=0), ahead_ref)
        return [
            (spec[i * blocks : (i + 1) * blocks, :rows], spec[i * blocks : (i + 1) * blocks, rows:])
            for i in range(len(signals))
        ]

    def inverse(spectra):
        parts = dot3(
            jnp.concatenate([jnp.concatenate(pair, axis=1) for pair in spectra], axis=0), back_ref
        )
        turned = []
        for i in range(len(spectra)):
            real = parts[i * blocks : (i + 1) * blocks, :rows]
            imag = parts[i * blocks : (i + 1) * blocks, rows:]
            turned.append(
                jnp.concatenate(
                    [real * cos_t - imag * sin_t, imag * cos_t + real * sin_t], axis=0
                )
            )
        high, low = split(jnp.concatenate(turned, axis=1))
        out = dot(last_ref[...], jnp.concatenate([high, high, low], axis=0))
        return [out[:, i * rows : (i + 1) * rows] for i in range(len(spectra))]

    for slot in range(slots):
        tap_row = slot // share * piece + 2 * slots + slot % share
        starts = [tap_row]
        for group in range(groups):
            starts += [group * piece + slot, group * piece + slots + slot]
        spectra = forward([data_ref[rows_of(start), :] for start in starts])
        filt_r, filt_i = spectra[0]
        tap_r, tap_i = 0.0, 0.0
        products = []
        for group in range(groups):
            prod_r, prod_i = spectra[1 + 2 * group]
            grad_r, grad_i = spectra[2 + 2 * group]
            products.append((prod_r * filt_r - prod_i * filt_i, prod_r * filt_i + prod_i * filt_r))
            products.append((grad_r * filt_r + grad_i * filt_i, grad_i * filt_r - grad_r * filt_i))
            tap_r = tap_r + (grad_r * prod_r + grad_i * prod_i)
            tap_i = tap_i + (grad_i * prod_r - grad_r * prod_i)
        for start, value in zip(starts, inverse([(tap_r, tap_i)] + products)):
            out_ref[rows_of(start), :] = value


def gates_kernel(
    slots, query_ref, key_ref, value_ref, grad_ref, skip_ref, data_ref, dq_ref, dk_ref, dv_ref
):
    rows, channels = query_ref.shape
    devices = channels // slots
    piece = data_ref.shape[0] // devices
    per = devices // rows
    for block in range(channels // rows):
        slot, start = block // per, block % per * rows * piece
        cols = pl.ds(block * rows, rows)
        conv = data_ref[pl.ds(start + slot, rows, stride=piece), :].T
        back = data_ref[pl.ds(start + slots + slot, rows, stride=piece), :].T
        key = key_ref[:, cols].astype(f32)
        value = value_ref[:, cols].astype(f32)
        grad = grad_ref[:, cols].astype(f32)
        skip = skip_ref[:, cols]
        mixed = conv + skip * (key * value)
        product_grad = back + skip * (query_ref[:, cols].astype(f32) * grad)
        dq_ref[:, cols] = (grad * mixed).astype(bf16)
        dk_ref[:, cols] = (product_grad * value).astype(bf16)
        dv_ref[:, cols] = (product_grad * key).astype(bf16)


def own_taps_kernel(slots, devices, data_ref, out_ref):
    rows = out_ref.shape[0]
    piece = data_ref.shape[0] // devices
    per = devices // rows
    for block in range(out_ref.shape[1] // rows):
        slot, start = block // per, block % per * rows * piece
        out_ref[:, pl.ds(block * rows, rows)] = data_ref[
            pl.ds(start + 2 * slots + slot, rows, stride=piece), :
        ].T


def join_kernel(grp_ref, *refs):
    width = refs[0].shape[1]
    for step, ref in enumerate(refs[:-1]):
        start = pl.multiple_of((grp_ref[0] ^ step) * width, 128)
        refs[-1][:, pl.ds(start, width)] = ref[...]


def local_call(kernel, out_shape, n_in, flops, moved, scalar=False):
    vmem = pl.BlockSpec(memory_space=pltpu.VMEM)
    specs = [pl.BlockSpec(memory_space=pltpu.SMEM)] if scalar else []
    return pl.pallas_call(
        kernel,
        out_shape=out_shape,
        in_specs=specs + [vmem] * n_in,
        out_specs=jax.tree.map(lambda _: vmem, out_shape),
        compiler_params=pltpu.CompilerParams(vmem_limit_bytes=48 * 2**20),
        cost_estimate=pl.CostEstimate(flops=flops, bytes_accessed=moved, transcendentals=0),
    )


def exchange(pieces, devices):
    flat = pieces.reshape(devices, 1, pieces.shape[0] // devices * pieces.shape[1])
    moved = lax.all_to_all(flat, ("seq", "grp"), split_axis=0, concat_axis=0, tiled=True)
    return moved.reshape(pieces.shape)


def body(query_gate, key_gate, value_in, grad_out, filter_taps, skip_gain):
    rows, channels = filter_taps.shape
    blocks, groups = lax.axis_size("seq"), lax.axis_size("grp")
    devices = blocks * groups
    slots = channels // devices
    share = slots // groups
    piece = 2 * slots + share
    width = share * devices
    grp = lax.axis_index("grp")
    gates = (query_gate[0], key_gate[0], value_in[0], grad_out[0])
    own = lax.dynamic_slice_in_dim(filter_taps, grp * width, width, 1)
    pieces = jax.ShapeDtypeStruct((devices * piece, rows), f32)
    size = devices * piece * rows * 4
    sent = local_call(functools.partial(pack_kernel, slots), pieces, 5, 0, 2 * size)(*gates, own)
    data = exchange(sent, devices)
    tables = [
        jnp.asarray(table)
        for table in transform_tables(blocks, rows, 1.0 / math.sqrt(blocks * rows))
    ]
    result = local_call(
        functools.partial(spectral_kernel, slots, groups, blocks), pieces, 6, 5 * 10**9, 2 * size
    )(data, *tables)
    back = exchange(result, devices)
    own_grad = local_call(
        functools.partial(own_taps_kernel, slots, devices),
        jax.ShapeDtypeStruct((rows, width), f32),
        1,
        0,
        rows * width * 8,
    )(back)
    parts = [own_grad] + [
        lax.ppermute(own_grad, "grp", [(i, i ^ step) for i in range(groups)])
        for step in range(1, groups)
    ]
    grad_shape = jax.ShapeDtypeStruct((rows, channels), bf16)
    query_grad, key_grad, value_grad = local_call(
        functools.partial(gates_kernel, slots), [grad_shape] * 3, 6, 0, 20 * size
    )(*gates, skip_gain[None], back)
    filter_grad = local_call(
        join_kernel, jax.ShapeDtypeStruct((rows, channels), f32), groups, 0, 2 * size, scalar=True
    )(grp.reshape(1), *parts)
    return (query_grad[None], key_grad[None], value_grad[None], filter_grad)


def solution(mesh):
    split_rows = P("grp", "seq", None)
    return jax.shard_map(
        body,
        mesh=mesh,
        in_specs=(split_rows,) * 4 + (P("seq", None), P()),
        out_specs=(split_rows,) * 3 + (P("seq", None),),
        check_vma=False,
    )
```

time: 734 us -> 174 us (0.24)
  waiting for transfers between devices: 444 us -> 10.4 us
  blocking collectives: 0 us -> 140 us
  local copies, waits for them, and re-layouts: 107 us -> 5.45 us
  starting transfers between devices: 76.6 us -> 2.23 us
  matrix products: 49.2 us -> 0 us
  other arithmetic: 37.8 us -> 0 us
  Pallas kernels: 0 us -> 14.8 us
  between operations: 14.5 us -> 0.77 us
    all_to_all x7 -> x0, waiting for transfers between devices: 294 us -> none  [the longest x1 54 us: forward_transform(): lax.all_to_all(pieces, 'seq', split_axis=0, concat_axis=0, tiled=True)]
    all_to_all x0 -> x2, blocking collectives: none -> 140 us  [exchange(): lax.all_to_all(flat, ('seq', 'grp'), split_axis=0, concat_axis=0, tiled=T...]
    all_gather x3 -> x0, waiting for transfers between devices: 84.9 us -> none  [the longest x1 35 us: body(): lax.all_gather(own_imag, 'grp', axis=2, tiled=True)]
    all_to_all x7 -> x0, starting transfers between devices: 75.7 us -> none  [the longest x1 15.8 us: forward_transform(): lax.all_to_all(pieces, 'seq', split_axis=0, concat_axis=0, tiled=True)]
    reduce_scatter x2 -> x0, waiting for transfers between devices: 65.2 us -> none  [the longest x1 34.3 us: body(): lax.psum_scatter(tap_imag, 'grp', scatter_dimension=2, tiled=True)]
    dot_general x14 -> x0, matrix products: 49.2 us -> none  [the longest x8 33.4 us: along_rows(): return jnp.einsum('kn,jnw->jkw', table, blocks, precision=highest)]
    slice x19 -> x0, local copies, waits for them, and re-layouts: 35.1 us -> none  [the longest x3 11.8 us: split_mirror(): jnp.roll(flip_imag[0], 1, axis=0)]
    rev x2 -> x0, local copies, waits for them, and re-layouts: 23.7 us -> none  [the longest x1 11.8 us: split_mirror(): flip_imag[::-1]]
  transfers between devices with their start and end apart: 12 -> 3, of which waited for: 12 -> 2; matrix products, arithmetic and copies ran while one was open for 5% -> 0% of each run, Pallas kernels for 0% -> 1%
where the time goes in v1:
time: 174 us; the launch traced here: 173 us
  blocking collectives  140 us (80%)
  Pallas kernels  14.8 us (9%)
  waiting for transfers between devices  10.4 us (6%)
  local copies, waits for them, and re-layouts  5.45 us (3%)
  starting transfers between devices  2.23 us (1%)
    all_to_all x2, blocking collectives, exchange(): lax.all_to_all(flat, ('seq', 'grp'), split_axis=0, concat_axis=0, tiled=T...  140 us
    pallas_call x1, Pallas kernels, body(): local_call(functools.partial(spectral_kernel, slots, groups, blocks), pie...  11.1 us
    ppermute x3, waiting for transfers between devices, body(): lax.ppermute(own_grad, 'grp', [(i, i ^ step) for i in range(groups)])  10.4 us
    unnamed x30, local copies, waits for them, and re-layouts  5.43 us
  transfers between devices with their start and end apart: 3, of which 2 were waited for; matrix products, arithmetic and copies ran while one was open for 0% of the time, Pallas kernels for 1%

profile of v1, /device:TPU:1, one launch (start us, length us, event | category | flops | bytes accessed | tf_op | source)
XLA Modules:
  0.0 173.3 jit_solution(13280012189770831765)
XLA Ops:
  0.6 0.0 copy-start
  0.7 1.2 copy-done
  1.9 1.0 copy-done.1
  2.9 1.0 copy-done.3
  4.0 1.0 copy-done.5
  5.0 1.0 copy-done.7
  6.1 0.7 shard_map.138
  6.7 0.0 copy-start.10
  6.8 0.0 copy-start.11
  6.8 0.0 copy-start.12
  6.8 0.0 copy-start.13
  6.8 0.0 copy-start.14
  6.8 74.6 %all_to_all.10 = f32[256,1,2304]{2,1,0:T(1,128)S(1)} all-to-all(f32[256,1,2304]{2,1,0:T(1,128)S(1)} %bitcast.15), channel_id=1, replica_groups=mesh['seq'=64,'grp'=4] {'seq','grp'}, dimensions={0} | all-to-all | bytes 4718592 | tf_op jit(solution)/shard_map/all_to_all | solution.py:195
  81.5 11.1 %shard_map.139 = f32[4608,128]{1,0:T(8,128)S(1)} custom-call(f32[4608,128]{1,0:T(8,128)S(1)} %bitcast.16, bf16[128,192]{1,0:T(8,128)(2,1)S(1)} %copy-done.13, f32[2,64,128]{2,1,0:T(8,128)S(1)} %copy-done.12, bf16[2,256,256]{2,1,0:T(8,128)(2,1)S(1)} %copy-done.11, bf16[2,256,256]{2,1,0:T(8,128)(2,1)S(1)} %copy-done.10, bf16[64,384]{1,0:T(8,128)(2,1)S(1)} %copy-done.14), custom_call_target="tpu_custom_call" | custom-call | flops 5000000000 | bytes 4718592 | tf_op jit(solution)/shard_map/pallas_call | solution.py:218
  92.6 65.0 %all_to_all.11 = f32[256,1,2304]{2,1,0:T(1,128)S(1)} all-to-all(f32[256,1,2304]{2,1,0:T(1,128)S(1)} %bitcast.17), channel_id=1, replica_groups=mesh['seq'=64,'grp'=4] {'seq','grp'}, dimensions={0} | all-to-all | bytes 4718592 | tf_op jit(solution)/shard_map/all_to_all | solution.py:195
  157.6 0.0 copy-start.9
  157.6 0.1 shard_map.141.refs_0_
  157.7 1.3 collective-permute-start.2
  159.0 0.8 collective-permute-start.1
  159.8 0.1 collective-permute-start
  160.0 1.9 %shard_map.140 = (bf16[128,2048]{1,0:T(8,128)(2,1)}, bf16[128,2048]{1,0:T(8,128)(2,1)}, bf16[128,2048]{1,0:T(8,128)(2,1)}) custom-call(bf16[128,2048]{1,0:T(8,128)(2,1)S(1)} %bitcast.19, bf16[128,2048]{1,0:T(8,128)(2,1)S(1)} %bitcast.21, bf16[128,2048]{1,0:T(8,128)(2,1)S(1)} %bitcast.23, bf16[128,2048]{1,0:T(8,128)(2,1)S(1)} %bitcast.25, ...), custom_call_target="tpu_custom_call" | custom-call | bytes 47185920 | tf_op jit(solution)/shard_map/pallas_call | solution.py:234
  161.9 4.7 %collective-permute-done.2.refs_3_ = f32[128,512]{1,0:T(8,128)S(1)} collective-permute-done((f32[128,512]{1,0:T(8,128)S(1)}, f32[128,512]{1,0:T(8,128)S(1)}, u32[]{:S(2)}, u32[]{:S(2)}) %collective-permute-start.2) | collective-permute-done | bytes 262176 | tf_op jit(solution)/shard_map/ppermute | solution.py:230
  166.6 5.6 %collective-permute-done.1.refs_2_ = f32[128,512]{1,0:T(8,128)S(1)} collective-permute-done((f32[128,512]{1,0:T(8,128)S(1)}, f32[128,512]{1,0:T(8,128)S(1)}, u32[]{:S(2)}, u32[]{:S(2)}) %collective-permute-start.1) | collective-permute-done | bytes 262176 | tf_op jit(solution)/shard_map/ppermute | solution.py:230
  172.2 1.0 shard_map.142
  (20 shorter events, 0.1 us)
Async XLA Ops:
  0.6 1.2 copy-start
  1.9 1.0 copy-start.1
  2.9 1.0 copy-start.3
  4.0 1.0 copy-start.5
  5.0 1.0 copy-start.7
  6.7 74.7 %copy-start.10 = (bf16[2,256,256]{2,1,0:T(8,128)(2,1)S(1)}, bf16[2,256,256]{2,1,0:T(8,128)(2,1)}, u32[]{:S(2)}) copy-start(bf16[2,256,256]{2,1,0:T(8,128)(2,1)} %constant.23.clone.back_ref) | copy-start | bytes 786436
  6.8 74.7 %copy-start.11 = (bf16[2,256,256]{2,1,0:T(8,128)(2,1)S(1)}, bf16[2,256,256]{2,1,0:T(8,128)(2,1)}, u32[]{:S(2)}) copy-start(bf16[2,256,256]{2,1,0:T(8,128)(2,1)} %constant.22.clone.ahead_ref) | copy-start | bytes 786436
  6.8 74.7 %copy-start.12 = (f32[2,64,128]{2,1,0:T(8,128)S(1)}, f32[2,64,128]{2,1,0:T(8,128)}, u32[]{:S(2)}) copy-start(f32[2,64,128]{2,1,0:T(8,128)} %constant.21.clone.turn_ref) | copy-start | bytes 196612
  6.8 74.7 %copy-start.13 = (bf16[128,192]{1,0:T(8,128)(2,1)S(1)}, bf16[128,192]{1,0:T(8,128)(2,1)}, u32[]{:S(2)}) copy-start(bf16[128,192]{1,0:T(8,128)(2,1)} %constant.20.clone.first_ref) | copy-start | bytes 147460
  6.8 74.7 %copy-start.14 = (bf16[64,384]{1,0:T(8,128)(2,1)S(1)}, bf16[64,384]{1,0:T(8,128)(2,1)}, u32[]{:S(2)}) copy-start(bf16[64,384]{1,0:T(8,128)(2,1)} %constant.24.clone.last_ref) | copy-start | bytes 147460
  157.6 2.4 %copy-start.2 = (bf16[1,128,2048]{2,1,0:T(8,128)(2,1)S(1)}, bf16[1,128,2048]{2,1,0:T(8,128)(2,1)}, u32[]{:S(2)}) copy-start(bf16[1,128,2048]{2,1,0:T(8,128)(2,1)} %param.11) | copy-start | bytes 1572868
  157.6 2.4 %copy-start.4 = (bf16[1,128,2048]{2,1,0:T(8,128)(2,1)S(1)}, bf16[1,128,2048]{2,1,0:T(8,128)(2,1)}, u32[]{:S(2)}) copy-start(bf16[1,128,2048]{2,1,0:T(8,128)(2,1)} %param.12) | copy-start | bytes 1572868
  157.6 2.4 %copy-start.6 = (bf16[1,128,2048]{2,1,0:T(8,128)(2,1)S(1)}, bf16[1,128,2048]{2,1,0:T(8,128)(2,1)}, u32[]{:S(2)}) copy-start(bf16[1,128,2048]{2,1,0:T(8,128)(2,1)} %param.13) | copy-start | bytes 1572868
  157.6 2.4 %copy-start.8 = (bf16[1,128,2048]{2,1,0:T(8,128)(2,1)S(1)}, bf16[1,128,2048]{2,1,0:T(8,128)(2,1)}, u32[]{:S(2)}) copy-start(bf16[1,128,2048]{2,1,0:T(8,128)(2,1)} %param.14) | copy-start | bytes 1572868
  157.6 2.4 %copy-start.9 = (f32[2048]{0:T(1024)S(1)}, f32[2048]{0:T(1024)}, u32[]{:S(2)}) copy-start(f32[2048]{0:T(1024)} %param.16) | copy-start | bytes 24580
  157.7 8.9 %collective-permute-start.2 = (f32[128,512]{1,0:T(8,128)S(1)}, f32[128,512]{1,0:T(8,128)S(1)}, u32[]{:S(2)}, u32[]{:S(2)}) collective-permute-start(f32[128,512]{1,0:T(8,128)S(1)} %shard_map.141.refs_0_), channel_id=1, source_target_pairs={{0,3},{1,2},{2,1},{3,0},{4,7},{5,6},{6,5},{7,4},{8,11},{9,10},{10,... | collective-permute-start | bytes 786440 | tf_op jit(solution)/shard_map/ppermute | solution.py:230
  159.0 13.2 %collective-permute-start.1 = (f32[128,512]{1,0:T(8,128)S(1)}, f32[128,512]{1,0:T(8,128)S(1)}, u32[]{:S(2)}, u32[]{:S(2)}) collective-permute-start(f32[128,512]{1,0:T(8,128)S(1)} %shard_map.141.refs_0_), channel_id=1, source_target_pairs={{0,2},{1,3},{2,0},{3,1},{4,6},{5,7},{6,4},{7,5},{8,10},{9,11},{10,... | collective-permute-start | bytes 786440 | tf_op jit(solution)/shard_map/ppermute | solution.py:230
  159.8 12.4 %collective-permute-start = (f32[128,512]{1,0:T(8,128)S(1)}, f32[128,512]{1,0:T(8,128)S(1)}, u32[]{:S(2)}, u32[]{:S(2)}) collective-permute-start(f32[128,512]{1,0:T(8,128)S(1)} %shard_map.141.refs_0_), channel_id=1, source_target_pairs={{0,1},{1,0},{2,3},{3,2},{4,5},{5,4},{6,7},{7,6},{8,9},{9,8},{10,11... | collective-permute-start | bytes 786440 | tf_op jit(solution)/shard_map/ppermute | solution.py:230

commit v2 on v1

--- a/solution.py
+++ b/solution.py
@@ -51,23 +51,42 @@
     return dot(high, table_ref[0]) + dot(low, table_ref[0]) + dot(high, table_ref[1])
 
 
-def pack_kernel(slots, query_ref, key_ref, value_ref, grad_ref, taps_ref, out_ref):
-    rows, channels = query_ref.shape
+def pack_kernel(slots, parts, grp_ref, *refs):
+    sources, taps_ref, out_ref, held, taps, sems, tap_sem = refs[:4], *refs[4:]
+    rows, channels = sources[0].shape
     devices = channels // slots
-    share = taps_ref.shape[1] // devices
+    share = taps.shape[1] // devices
     piece = 2 * slots + share
     per = devices // rows
+    width = channels // parts
+    copies = []
+    for part in range(parts):
+        cols = pl.ds(part * width, width)
+        copies.append(
+            [
+                pltpu.make_async_copy(ref.at[:, cols], held.at[i, :, cols], sems.at[i, part])
+                for i, ref in enumerate(sources)
+            ]
+        )
+        for copy in copies[-1]:
+            copy.start()
+    start = pl.multiple_of(grp_ref[0] * taps.shape[1], 128)
+    tap_copy = pltpu.make_async_copy(taps_ref.at[:, pl.ds(start, taps.shape[1])], taps, tap_sem)
+    tap_copy.start()
     for block in range(channels // rows):
+        if block * rows % width == 0:
+            for copy in copies[block * rows // width]:
+                copy.wait()
         slot, start = block // per, block % per * rows * piece
         cols = pl.ds(block * rows, rows)
-        product = key_ref[:, cols].astype(f32) * value_ref[:, cols].astype(f32)
-        gated = query_ref[:, cols].astype(f32) * grad_ref[:, cols].astype(f32)
-        out_ref[pl.ds(start + slot, rows, stride=piece), :] = product.T
-        out_ref[pl.ds(start + slots + slot, rows, stride=piece), :] = gated.T
+        query, key, value, grad = (held[i, :, cols].astype(f32) for i in range(4))
+        out_ref[pl.ds(start + slot, rows, stride=piece), :] = (key * value).T
+        out_ref[pl.ds(start + slots + slot, rows, stride=piece), :] = (query * grad).T
+    tap_copy.wait()
     for block in range(share * per):
         slot, start = block // per, block % per * rows * piece
-        taps = taps_ref[:, pl.ds(block * rows, rows)]
-        out_ref[pl.ds(start + 2 * slots + slot, rows, stride=piece), :] = taps.T
+        own = taps[:, pl.ds(block * rows, rows)]
+        out_ref[pl.ds(start + 2 * slots + slot, rows, stride=piece), :] = own.T
 
 
 def spectral_kernel(
@@ -84,6 +103,7 @@
     def forward(signals):
         high, low = split(jnp.concatenate(signals, axis=1))
         freq = dot(first_ref[...], jnp.concatenate([high, high, low], axis=0))
+        yield
         turned = []
         for i in range(len(signals)):
             real = freq[:blocks, i * rows : (i + 1) * rows]
@@ -93,8 +113,9 @@
                     [real * cos_t + imag * sin_t, imag * cos_t - real * sin_t], axis=1
                 )
             )
+        yield
         spec = dot3(jnp.concatenate(turned, axis=0), ahead_ref)
-        return [
+        yield [
             (spec[i * blocks : (i + 1) * blocks, :rows], spec[i * blocks : (i + 1) * blocks, rows:])
             for i in range(len(signals))
         ]
@@ -103,6 +124,7 @@
         parts = dot3(
             jnp.concatenate([jnp.concatenate(pair, axis=1) for pair in spectra], axis=0), back_ref
         )
+        yield
         turned = []
         for i in range(len(spectra)):
             real = parts[i * blocks : (i + 1) * blocks, :rows]
@@ -112,16 +134,18 @@
                     [real * cos_t - imag * sin_t, imag * cos_t + real * sin_t], axis=0
                 )
             )
+        yield
         high, low = split(jnp.concatenate(turned, axis=1))
         out = dot(last_ref[...], jnp.concatenate([high, high, low], axis=0))
-        return [out[:, i * rows : (i + 1) * rows] for i in range(len(spectra))]
-
-    for slot in range(slots):
-        tap_row = slot // share * piece + 2 * slots + slot % share
-        starts = [tap_row]
+        yield [out[:, i * rows : (i + 1) * rows] for i in range(len(spectra))]
+
+    def starts_of(slot):
+        starts = [slot // share * piece + 2 * slots + slot % share]
         for group in range(groups):
             starts += [group * piece + slot, group * piece + slots + slot]
-        spectra = forward([data_ref[rows_of(start), :] for start in starts])
+        return starts
+
+    def products_of(spectra):
         filt_r, filt_i = spectra[0]
         tap_r, tap_i = 0.0, 0.0
         products = []
@@ -132,8 +156,23 @@
             products.append((grad_r * filt_r + grad_i * filt_i, grad_i * filt_r - grad_r * filt_i))
             tap_r = tap_r + (grad_r * prod_r + grad_i * prod_i)
             tap_i = tap_i + (grad_i * prod_r - grad_r * prod_i)
-        for start, value in zip(starts, inverse([(tap_r, tap_i)] + products)):
-            out_ref[rows_of(start), :] = value
+        return [(tap_r, tap_i)] + products
+
+    before = None
+    for slot in range(slots + 1):
+        steps = []
+        if slot < slots:
+            steps.append(forward([data_ref[rows_of(start), :] for start in starts_of(slot)]))
+        if before is not None:
+            steps.append(inverse(before))
+        for _ in range(2):
+            for step in steps:
+                next(step)
+        results = [next(step) for step in steps]
+        if before is not None:
+            for start, value in zip(starts_of(slot - 1), results[-1]):
+                out_ref[rows_of(start), :] = value
+        before = products_of(results[0]) if slot < slots else None
 
 
 def gates_kernel(
@@ -206,10 +245,27 @@
     width = share * devices
     grp = lax.axis_index("grp")
     gates = (query_gate[0], key_gate[0], value_in[0], grad_out[0])
-    own = lax.dynamic_slice_in_dim(filter_taps, grp * width, width, 1)
     pieces = jax.ShapeDtypeStruct((devices * piece, rows), f32)
     size = devices * piece * rows * 4
-    sent = local_call(functools.partial(pack_kernel, slots), pieces, 5, 0, 2 * size)(*gates, own)
+    parts = 4
+    sent = pl.pallas_call(
+        functools.partial(pack_kernel, slots, parts),
+        out_shape=pieces,
+        in_specs=[pl.BlockSpec(memory_space=pltpu.SMEM)]
+        + [pl.BlockSpec(memory_space=pltpu.HBM)] * 5,
+        out_specs=pl.BlockSpec(memory_space=pltpu.VMEM),
+        scratch_shapes=[
+            pltpu.VMEM((4, rows, channels), bf16),
+            pltpu.VMEM((rows, width), f32),
+            pltpu.SemaphoreType.DMA((4, parts)),
+            pltpu.SemaphoreType.DMA,
+        ],
+        compiler_params=pltpu.CompilerParams(vmem_limit_bytes=48 * 2**20),
+        cost_estimate=pl.CostEstimate(flops=0, bytes_accessed=2 * size, transcendentals=0),
+    )(
+        grp.reshape(1),
+        *(pltpu.with_memory_space_constraint(ref, pltpu.HBM) for ref in (*gates, filter_taps)),
+    )
     data = exchange(sent, devices)
     tables = [
         jnp.asarray(table)
@@ -226,10 +282,10 @@
         0,
         rows * width * 8,
     )(back)
-    parts = [own_grad] + [
-        lax.ppermute(own_grad, "grp", [(i, i ^ step) for i in range(groups)])
-        for step in range(1, groups)
-    ]
+    flip_core, flip_chip = ([(i, i ^ step) for i in range(groups)] for step in (1, 2))
+    across = lax.ppermute(own_grad, "grp", flip_chip)
+    beside = lax.ppermute(own_grad, "grp", flip_core)
+    parts = [own_grad, beside, across, lax.ppermute(across, "grp", flip_core)]
     grad_shape = jax.ShapeDtypeStruct((rows, channels), bf16)
     query_grad, key_grad, value_grad = local_call(
         functools.partial(gates_kernel, slots), [grad_shape] * 3, 6, 0, 20 * size

time: 174 us -> 162 us (0.931)
  local copies, waits for them, and re-layouts: 5.45 us -> 0.06 us
  waiting for transfers between devices: 10.4 us -> 5.62 us
  Pallas kernels: 14.8 us -> 12.7 us
    unnamed x30 -> x20, local copies, waits for them, and re-layouts: 5.43 us -> 0.06 us
    ppermute x3, waiting for transfers between devices: 10.4 us -> 5.62 us  [the longest x1 5.62 us: body(): across = lax.ppermute(own_grad, 'grp', flip_chip)]
    pallas_call x1, Pallas kernels: 11.1 us -> 7.29 us  [body(): local_call(functools.partial(spectral_kernel, slots, groups, blocks), pie...]
  transfers between devices with their start and end apart: 3 -> 3, of which waited for: 2 -> 1; matrix products, arithmetic and copies ran while one was open for 0% -> 0% of each run, Pallas kernels for 1% -> 1%
where the time goes in v2:
time: 162 us
  blocking collectives  140 us (86%)
  Pallas kernels  12.7 us (8%)
  waiting for transfers between devices  5.62 us (3%)
  starting transfers between devices  3.19 us (2%)
    all_to_all x2, blocking collectives, exchange(): lax.all_to_all(flat, ('seq', 'grp'), split_axis=0, concat_axis=0, tiled=T...  140 us
    pallas_call x1, Pallas kernels, body(): local_call(functools.partial(spectral_kernel, slots, groups, blocks), pie...  7.29 us
    ppermute x1, waiting for transfers between devices, body(): across = lax.ppermute(own_grad, 'grp', flip_chip)  5.62 us
  transfers between devices with their start and end apart: 3, of which 1 were waited for; matrix products, arithmetic and copies ran while one was open for 0% of the time, Pallas kernels for 1%

profile of v2, /device:TPU:1, one launch (start us, length us, event | category | flops | bytes accessed | tf_op | source)
XLA Modules:
  0.0 161.9 jit_solution(16613008942433088288)
XLA Ops:
  0.6 2.3 %shard_map.138 = f32[4608,128]{1,0:T(8,128)S(1)} custom-call(s32[1]{0:T(128)} %bitcast.5.grp_ref, bf16[128,2048]{1,0:T(8,128)(2,1)} %bitcast.18, bf16[128,2048]{1,0:T(8,128)(2,1)} %bitcast.20, bf16[128,2048]{1,0:T(8,128)(2,1)} %bitcast.22, bf16[128,2048]{1,0:T(8,128)(2,1)} %bitcast.24, f32[128,2048]{1,0:T(8,128)} %refs_4_.1), custom_call_target="tpu_custom_call" | custom-call | bytes 4718592 | tf_op jit(solution)/shard_map/pallas_call | solution.py:251
  2.9 0.0 copy-start.5
  2.9 0.0 copy-start.6
  3.0 0.0 copy-start.7
  3.0 0.0 copy-start.8
  3.0 0.0 copy-start.9
  3.0 74.6 %all_to_all.10 = f32[256,1,2304]{2,1,0:T(1,128)S(1)} all-to-all(f32[256,1,2304]{2,1,0:T(1,128)S(1)} %bitcast.15), channel_id=1, replica_groups=mesh['seq'=64,'grp'=4] {'seq','grp'}, dimensions={0} | all-to-all | bytes 4718592 | tf_op jit(solution)/shard_map/all_to_all | solution.py:234
  77.6 0.0 copy-done.5
  77.6 0.0 copy-done.6
  77.6 0.0 copy-done.7
  77.7 7.3 %shard_map.139 = f32[4608,128]{1,0:T(8,128)S(1)} custom-call(f32[4608,128]{1,0:T(8,128)S(1)} %bitcast.16, bf16[128,192]{1,0:T(8,128)(2,1)S(1)} %copy-done.8, f32[2,64,128]{2,1,0:T(8,128)S(1)} %copy-done.7, bf16[2,256,256]{2,1,0:T(8,128)(2,1)S(1)} %copy-done.6, bf16[2,256,256]{2,1,0:T(8,128)(2,1)S(1)} %copy-done.5, bf16[64,384]{1,0:T(8,128)(2,1)S(1)} %copy-done.9), custom_call_target="tpu_custom_call" | custom-call | flops 5000000000 | bytes 4718592 | tf_op jit(solution)/shard_map/pallas_call | solution.py:274
  85.0 65.0 %all_to_all.11 = f32[256,1,2304]{2,1,0:T(1,128)S(1)} all-to-all(f32[256,1,2304]{2,1,0:T(1,128)S(1)} %bitcast.17), channel_id=1, replica_groups=mesh['seq'=64,'grp'=4] {'seq','grp'}, dimensions={0} | all-to-all | bytes 4718592 | tf_op jit(solution)/shard_map/all_to_all | solution.py:234
  150.0 0.0 copy-start.4
  150.0 0.1 shard_map.141.refs_0_
  150.1 0.2 collective-permute-start.1
  150.3 1.5 collective-permute-start
  151.8 5.6 %collective-permute-done.1.refs_2_ = f32[128,512]{1,0:T(8,128)S(1)} collective-permute-done((f32[128,512]{1,0:T(8,128)S(1)}, f32[128,512]{1,0:T(8,128)S(1)}, u32[]{:S(2)}, u32[]{:S(2)}) %collective-permute-start.1) | collective-permute-done | bytes 262176 | tf_op jit(solution)/shard_map/ppermute | solution.py:286
  157.4 1.5 collective-permute-start.2
  158.9 0.0 copy-done
  158.9 0.0 copy-done.4
  158.9 1.9 %shard_map.140 = (bf16[128,2048]{1,0:T(8,128)(2,1)}, bf16[128,2048]{1,0:T(8,128)(2,1)}, bf16[128,2048]{1,0:T(8,128)(2,1)}) custom-call(bf16[128,2048]{1,0:T(8,128)(2,1)S(1)} %bitcast.19, bf16[128,2048]{1,0:T(8,128)(2,1)S(1)} %bitcast.21, bf16[128,2048]{1,0:T(8,128)(2,1)S(1)} %bitcast.23, bf16[128,2048]{1,0:T(8,128)(2,1)S(1)} %bitcast.25, ...), custom_call_target="tpu_custom_call" | custom-call | bytes 47185920 | tf_op jit(solution)/shard_map/pallas_call | solution.py:290
  160.8 0.0 collective-permute-done.refs_1_
  160.8 0.0 collective-permute-done.2.refs_3_
  160.8 1.0 shard_map.142
  (9 shorter events, 0.0 us)
Async XLA Ops:
  2.9 74.7 %copy-start.5 = (bf16[2,256,256]{2,1,0:T(8,128)(2,1)S(1)}, bf16[2,256,256]{2,1,0:T(8,128)(2,1)}, u32[]{:S(2)}) copy-start(bf16[2,256,256]{2,1,0:T(8,128)(2,1)} %constant.17.clone.back_ref) | copy-start | bytes 786436
  2.9 74.7 %copy-start.6 = (bf16[2,256,256]{2,1,0:T(8,128)(2,1)S(1)}, bf16[2,256,256]{2,1,0:T(8,128)(2,1)}, u32[]{:S(2)}) copy-start(bf16[2,256,256]{2,1,0:T(8,128)(2,1)} %constant.16.clone.ahead_ref) | copy-start | bytes 786436
  3.0 74.7 %copy-start.7 = (f32[2,64,128]{2,1,0:T(8,128)S(1)}, f32[2,64,128]{2,1,0:T(8,128)}, u32[]{:S(2)}) copy-start(f32[2,64,128]{2,1,0:T(8,128)} %constant.15.clone.turn_ref) | copy-start | bytes 196612
  3.0 74.7 %copy-start.8 = (bf16[128,192]{1,0:T(8,128)(2,1)S(1)}, bf16[128,192]{1,0:T(8,128)(2,1)}, u32[]{:S(2)}) copy-start(bf16[128,192]{1,0:T(8,128)(2,1)} %constant.14.clone.first_ref) | copy-start | bytes 147460
  3.0 74.7 %copy-start.9 = (bf16[64,384]{1,0:T(8,128)(2,1)S(1)}, bf16[64,384]{1,0:T(8,128)(2,1)}, u32[]{:S(2)}) copy-start(bf16[64,384]{1,0:T(8,128)(2,1)} %constant.18.clone.last_ref) | copy-start | bytes 147460
  149.9 9.0 %copy-start = (bf16[1,128,2048]{2,1,0:T(8,128)(2,1)S(1)}, bf16[1,128,2048]{2,1,0:T(8,128)(2,1)}, u32[]{:S(2)}) copy-start(bf16[1,128,2048]{2,1,0:T(8,128)(2,1)} %param.11) | copy-start | bytes 1572868
  149.9 9.0 %copy-start.1 = (bf16[1,128,2048]{2,1,0:T(8,128)(2,1)S(1)}, bf16[1,128,2048]{2,1,0:T(8,128)(2,1)}, u32[]{:S(2)}) copy-start(bf16[1,128,2048]{2,1,0:T(8,128)(2,1)} %param.12) | copy-start | bytes 1572868
  149.9 9.0 %copy-start.2 = (bf16[1,128,2048]{2,1,0:T(8,128)(2,1)S(1)}, bf16[1,128,2048]{2,1,0:T(8,128)(2,1)}, u32[]{:S(2)}) copy-start(bf16[1,128,2048]{2,1,0:T(8,128)(2,1)} %param.13) | copy-start | bytes 1572868
  150.0 9.0 %copy-start.3 = (bf16[1,128,2048]{2,1,0:T(8,128)(2,1)S(1)}, bf16[1,128,2048]{2,1,0:T(8,128)(2,1)}, u32[]{:S(2)}) copy-start(bf16[1,128,2048]{2,1,0:T(8,128)(2,1)} %param.14) | copy-start | bytes 1572868
  150.0 9.0 %copy-start.4 = (f32[2048]{0:T(1024)S(1)}, f32[2048]{0:T(1024)}, u32[]{:S(2)}) copy-start(f32[2048]{0:T(1024)} %param.16) | copy-start | bytes 24580
  150.1 7.3 %collective-permute-start.1 = (f32[128,512]{1,0:T(8,128)S(1)}, f32[128,512]{1,0:T(8,128)S(1)}, u32[]{:S(2)}, u32[]{:S(2)}) collective-permute-start(f32[128,512]{1,0:T(8,128)S(1)} %shard_map.141.refs_0_), channel_id=1, source_target_pairs={{0,2},{1,3},{2,0},{3,1},{4,6},{5,7},{6,4},{7,5},{8,10},{9,11},{10,... | collective-permute-start | bytes 786440 | tf_op jit(solution)/shard_map/ppermute | solution.py:286
  150.3 10.5 %collective-permute-start = (f32[128,512]{1,0:T(8,128)S(1)}, f32[128,512]{1,0:T(8,128)S(1)}, u32[]{:S(2)}, u32[]{:S(2)}) collective-permute-start(f32[128,512]{1,0:T(8,128)S(1)} %shard_map.141.refs_0_), channel_id=1, source_target_pairs={{0,1},{1,0},{2,3},{3,2},{4,5},{5,4},{6,7},{7,6},{8,9},{9,8},{10,11... | collective-permute-start | bytes 786440 | tf_op jit(solution)/shard_map/ppermute | solution.py:287
  157.4 3.4 %collective-permute-start.2 = (f32[128,512]{1,0:T(8,128)S(1)}, f32[128,512]{1,0:T(8,128)S(1)}, u32[]{:S(2)}, u32[]{:S(2)}) collective-permute-start(f32[128,512]{1,0:T(8,128)S(1)} %collective-permute-done.1.refs_2_), channel_id=1, source_target_pairs={{0,1},{1,0},{2,3},{3,2},{4,5},{5,4},{6,7},{7,6},{8,9},{9,8},{10,11... | collective-permute-start | bytes 786440 | tf_op jit(solution)/shard_map/ppermute | solution.py:288

commit v3 on v2

--- a/solution.py
+++ b/solution.py
@@ -30,11 +30,12 @@
     ahead1 = halves(np.concatenate([c1, -s1], axis=0))
     ahead2 = halves(np.block([[c2, -s2], [s2, c2]]))
     back2 = halves(np.block([[c2, s2], [-s2, c2]]))
+    ahead2, back2 = (np.concatenate([h, h, l], axis=0) for h, l in (ahead2, back2))
     back1 = halves(np.concatenate([c1.T, -s1.T], axis=1) * (2.0 * scale / full))
     stack1 = np.concatenate([ahead1[0], ahead1[1], ahead1[0]], axis=1)
     unstack1 = np.concatenate([back1[0], back1[1], back1[0]], axis=1)
     turn = np.stack([np.cos(twist), np.sin(twist)]).astype(np.float32)
-    return stack1, turn, np.stack(ahead2), np.stack(back2), unstack1
+    return stack1, turn, ahead2, back2, unstack1
 
 
 def split(value):
@@ -48,7 +49,7 @@
 
 def dot3(value, table_ref):
     high, low = split(value)
-    return dot(high, table_ref[0]) + dot(low, table_ref[0]) + dot(high, table_ref[1])
+    return dot(jnp.concatenate([high, low, high], axis=1), table_ref[...])
 
 
 def pack_kernel(slots, parts, grp_ref, *refs):
@@ -198,22 +199,45 @@
         dv_ref[:, cols] = (product_grad * key).astype(bf16)
 
 
-def own_taps_kernel(slots, devices, data_ref, out_ref):
-    rows = out_ref.shape[0]
+def own_taps_kernel(slots, devices, data_ref, *out_refs):
+    rows, width = out_refs[0].shape
     piece = data_ref.shape[0] // devices
-    per = devices // rows
-    for block in range(out_ref.shape[1] // rows):
-        slot, start = block // per, block % per * rows * piece
-        out_ref[:, pl.ds(block * rows, rows)] = data_ref[
-            pl.ds(start + 2 * slots + slot, rows, stride=piece), :
-        ].T
-
-
-def join_kernel(grp_ref, *refs):
-    width = refs[0].shape[1]
-    for step, ref in enumerate(refs[:-1]):
-        start = pl.multiple_of((grp_ref[0] ^ step) * width, 128)
-        refs[-1][:, pl.ds(start, width)] = ref[...]
+    for slot, out_ref in enumerate(out_refs):
+        for block in range(width // rows):
+            start = block * rows * piece + 2 * slots + slot
+            out_ref[:, pl.ds(block * rows, rows)] = data_ref[pl.ds(start, rows, stride=piece), :].T
+
+
+def join_kernel(share, places, fresh, grp_ref, *refs):
+    blocks, out_ref, sems = refs[0 if fresh else 1 :][: len(places)], *refs[-2:]
+    width = blocks[0].shape[1]
+    writes = []
+    for i, (flip, slot) in enumerate(places):
+        start = pl.multiple_of(((grp_ref[0] ^ flip) * share + slot) * width, 128)
+        writes.append(
+            pltpu.make_async_copy(blocks[i], out_ref.at[:, pl.ds(start, width)], sems.at[i])
+        )
+    for write in writes:
+        write.start()
+    for write in writes:
+        write.wait()
+
+
+def join(grp, known, places, shape, share, begun=None):
+    hbm = pl.BlockSpec(memory_space=pltpu.HBM)
+    before = [] if begun is None else [begun]
+    return pl.pallas_call(
+        functools.partial(join_kernel, share, places, begun is None),
+        out_shape=shape,
+        in_specs=[pl.BlockSpec(memory_space=pltpu.SMEM)]
+        + [hbm] * len(before)
+        + [pl.BlockSpec(memory_space=pltpu.VMEM)] * len(places),
+        out_specs=hbm,
+        scratch_shapes=[pltpu.SemaphoreType.DMA((len(places),))],
+        input_output_aliases={} if begun is None else {1: 0},
+        compiler_params=pltpu.CompilerParams(vmem_limit_bytes=48 * 2**20),
+        cost_estimate=pl.CostEstimate(flops=0, bytes_accessed=2**21, transcendentals=0),
+    )(grp.reshape(1), *before, *(known[place] for place in places))
 
 
 def local_call(kernel, out_shape, n_in, flops, moved, scalar=False):
@@ -275,24 +299,32 @@
         functools.partial(spectral_kernel, slots, groups, blocks), pieces, 6, 5 * 10**9, 2 * size
     )(data, *tables)
     back = exchange(result, devices)
-    own_grad = local_call(
+    own = local_call(
         functools.partial(own_taps_kernel, slots, devices),
-        jax.ShapeDtypeStruct((rows, width), f32),
+        [jax.ShapeDtypeStruct((rows, devices), f32)] * share,
         1,
         0,
         rows * width * 8,
     )(back)
     flip_core, flip_chip = ([(i, i ^ step) for i in range(groups)] for step in (1, 2))
-    across = lax.ppermute(own_grad, "grp", flip_chip)
-    beside = lax.ppermute(own_grad, "grp", flip_core)
-    parts = [own_grad, beside, across, lax.ppermute(across, "grp", flip_core)]
+    across = [lax.ppermute(part, "grp", flip_chip) for part in own]
+    beside = [lax.ppermute(part, "grp", flip_core) for part in own]
     grad_shape = jax.ShapeDtypeStruct((rows, channels), bf16)
     query_grad, key_grad, value_grad = local_call(
         functools.partial(gates_kernel, slots), [grad_shape] * 3, 6, 0, 20 * size
     )(*gates, skip_gain[None], back)
-    filter_grad = local_call(
-        join_kernel, jax.ShapeDtypeStruct((rows, channels), f32), groups, 0, 2 * size, scalar=True
-    )(grp.reshape(1), *parts)
+    across[0], query_grad = lax.optimization_barrier((across[0], query_grad))
+    known = {}
+    for slot in range(share):
+        known[0, slot], known[1, slot], known[2, slot] = own[slot], beside[slot], across[slot]
+    known[3, 0] = lax.ppermute(across[0], "grp", flip_core)
+    filter_shape = jax.ShapeDtypeStruct((rows, channels), f32)
+    early = [(flip, slot) for flip in (0, 1) for slot in range(share)] + [(2, 0)]
+    begun = join(grp, known, early, filter_shape, share)
+    known[2, 1], begun = lax.optimization_barrier((known[2, 1], begun))
+    known[3, 1] = lax.ppermute(known[2, 1], "grp", flip_core)
+    late = [(3, 0), (2, 1), (3, 1)]
+    filter_grad = join(grp, known, late, filter_shape, share, begun)
     return (query_grad[None], key_grad[None], value_grad[None], filter_grad)
 
 

time: 162 us -> 161 us (level)
  waiting for transfers between devices: 5.62 us -> 1.08 us
  starting transfers between devices: 3.19 us -> 5.9 us
    ppermute x3 -> x6, waiting for transfers between devices: 5.62 us -> 1.08 us  [the longest x1 0.98 us: body(): known[3, 1] = lax.ppermute(known[2, 1], 'grp', flip_core)]
    ppermute x3 -> x6, starting transfers between devices: 3.19 us -> 5.9 us  [the longest x1 2.62 us: body(): known[3, 0] = lax.ppermute(across[0], 'grp', flip_core)]
  transfers between devices with their start and end apart: 3 -> 6, of which waited for: 1 -> 2; matrix products, arithmetic and copies ran while one was open for 0% -> 0% of each run, Pallas kernels for 1% -> 2%
where the time goes in v3:
time: 161 us; the launch traced here: 160 us
  blocking collectives  140 us (87%)
  Pallas kernels  13.1 us (8%)
  starting transfers between devices  5.9 us (4%)
    all_to_all x2, blocking collectives, exchange(): lax.all_to_all(flat, ('seq', 'grp'), split_axis=0, concat_axis=0, tiled=T...  140 us
    pallas_call x1, Pallas kernels, body(): local_call(functools.partial(spectral_kernel, slots, groups, blocks), pie...  7.12 us
  transfers between devices with their start and end apart: 6, of which 2 were waited for; matrix products, arithmetic and copies ran while one was open for 0% of the time, Pallas kernels for 2%

profile of v3, /device:TPU:1, one launch (start us, length us, event | category | flops | bytes accessed | tf_op | source)
XLA Modules:
  0.0 160.5 jit_solution(17978832192392625806)
XLA Ops:
  0.6 2.3 %shard_map.138 = f32[4608,128]{1,0:T(8,128)S(1)} custom-call(s32[1]{0:T(128)} %bitcast.grp_ref, bf16[128,2048]{1,0:T(8,128)(2,1)} %bitcast.18, bf16[128,2048]{1,0:T(8,128)(2,1)} %bitcast.20, bf16[128,2048]{1,0:T(8,128)(2,1)} %bitcast.22, bf16[128,2048]{1,0:T(8,128)(2,1)} %bitcast.24, f32[128,2048]{1,0:T(8,128)} %refs_4_.1), custom_call_target="tpu_custom_call" | custom-call | bytes 4718592 | tf_op jit(solution)/shard_map/pallas_call | solution.py:275
  2.9 0.0 copy-start.5
  2.9 0.0 copy-start.6
  3.0 0.0 copy-start.7
  3.0 0.0 copy-start.8
  3.0 0.0 copy-start.9
  3.0 74.6 %all_to_all.10 = f32[256,1,2304]{2,1,0:T(1,128)S(1)} all-to-all(f32[256,1,2304]{2,1,0:T(1,128)S(1)} %bitcast.15), channel_id=1, replica_groups=mesh['seq'=64,'grp'=4] {'seq','grp'}, dimensions={0} | all-to-all | bytes 4718592 | tf_op jit(solution)/shard_map/all_to_all | solution.py:258
  77.7 7.1 %shard_map.139 = f32[4608,128]{1,0:T(8,128)S(1)} custom-call(f32[4608,128]{1,0:T(8,128)S(1)} %bitcast.16, bf16[128,192]{1,0:T(8,128)(2,1)S(1)} %copy-done.8, f32[2,64,128]{2,1,0:T(8,128)S(1)} %copy-done.7, bf16[768,256]{1,0:T(8,128)(2,1)S(1)} %copy-done.6, bf16[768,256]{1,0:T(8,128)(2,1)S(1)} %copy-done.5, bf16[64,384]{1,0:T(8,128)(2,1)S(1)} %copy-done.9), custom_call_target="tpu_custom_call" | custom-call | flops 5000000000 | bytes 4718592 | tf_op jit(solution)/shard_map/pallas_call | solution.py:298
  84.8 65.0 %all_to_all.11 = f32[256,1,2304]{2,1,0:T(1,128)S(1)} all-to-all(f32[256,1,2304]{2,1,0:T(1,128)S(1)} %bitcast.17), channel_id=1, replica_groups=mesh['seq'=64,'grp'=4] {'seq','grp'}, dimensions={0} | all-to-all | bytes 4718592 | tf_op jit(solution)/shard_map/all_to_all | solution.py:258
  149.8 0.0 copy-start.4
  149.8 0.1 shard_map.140
  149.9 0.2 collective-permute-start
  150.1 1.5 collective-permute-start.2
  151.6 0.0 collective-permute-start.3
  151.6 0.8 collective-permute-start.1
  152.4 1.9 %shard_map.141 = (bf16[128,2048]{1,0:T(8,128)(2,1)}, bf16[128,2048]{1,0:T(8,128)(2,1)}, bf16[128,2048]{1,0:T(8,128)(2,1)}) custom-call(bf16[128,2048]{1,0:T(8,128)(2,1)S(1)} %bitcast.19, bf16[128,2048]{1,0:T(8,128)(2,1)S(1)} %bitcast.21, bf16[128,2048]{1,0:T(8,128)(2,1)S(1)} %bitcast.23, bf16[128,2048]{1,0:T(8,128)(2,1)S(1)} %bitcast.25, ...), custom_call_target="tpu_custom_call" | custom-call | bytes 47185920 | tf_op jit(solution)/shard_map/pallas_call | solution.py:313
  154.3 0.1 collective-permute-done.refs_4_
  154.4 2.6 %collective-permute-start.4 = (f32[128,256]{1,0:T(8,128)S(1)}, f32[128,256]{1,0:T(8,128)S(1)}, u32[]{:S(2)}, u32[]{:S(2)}) collective-permute-start(f32[128,256]{1,0:T(8,128)S(1)} %collective-permute-done.refs_4_), channel_id=1, source_target_pairs={{0,1},{1,0},{2,3},{3,2},{4,5},{5,4},{6,7},{7,6},{8,9},{9,8},{10,11... | collective-permute-start | bytes 393224 | tf_op jit(solution)/shard_map/ppermute | solution.py:320
  157.0 0.0 collective-permute-done.2.refs_2_
  157.1 0.9 shard_map.142.refs_0_
  157.9 0.8 collective-permute-start.5
  158.7 0.0 collective-permute-done.4.refs_1_
  158.7 1.0 collective-permute-done.5.refs_3_
  159.7 0.8 shard_map.143
  (16 shorter events, 0.0 us)
Async XLA Ops:
  2.9 74.7 %copy-start.5 = (bf16[768,256]{1,0:T(8,128)(2,1)S(1)}, bf16[768,256]{1,0:T(8,128)(2,1)}, u32[]{:S(2)}) copy-start(bf16[768,256]{1,0:T(8,128)(2,1)} %constant.17.clone.back_ref) | copy-start | bytes 1179652
  2.9 74.7 %copy-start.6 = (bf16[768,256]{1,0:T(8,128)(2,1)S(1)}, bf16[768,256]{1,0:T(8,128)(2,1)}, u32[]{:S(2)}) copy-start(bf16[768,256]{1,0:T(8,128)(2,1)} %constant.16.clone.ahead_ref) | copy-start | bytes 1179652
  3.0 74.7 %copy-start.7 = (f32[2,64,128]{2,1,0:T(8,128)S(1)}, f32[2,64,128]{2,1,0:T(8,128)}, u32[]{:S(2)}) copy-start(f32[2,64,128]{2,1,0:T(8,128)} %constant.15.clone.turn_ref) | copy-start | bytes 196612
  3.0 74.7 %copy-start.8 = (bf16[128,192]{1,0:T(8,128)(2,1)S(1)}, bf16[128,192]{1,0:T(8,128)(2,1)}, u32[]{:S(2)}) copy-start(bf16[128,192]{1,0:T(8,128)(2,1)} %constant.14.clone.first_ref) | copy-start | bytes 147460
  3.0 74.7 %copy-start.9 = (bf16[64,384]{1,0:T(8,128)(2,1)S(1)}, bf16[64,384]{1,0:T(8,128)(2,1)}, u32[]{:S(2)}) copy-start(bf16[64,384]{1,0:T(8,128)(2,1)} %constant.18.clone.last_ref) | copy-start | bytes 147460
  149.8 2.6 %copy-start = (bf16[1,128,2048]{2,1,0:T(8,128)(2,1)S(1)}, bf16[1,128,2048]{2,1,0:T(8,128)(2,1)}, u32[]{:S(2)}) copy-start(bf16[1,128,2048]{2,1,0:T(8,128)(2,1)} %param.11) | copy-start | bytes 1572868
  149.8 2.6 %copy-start.1 = (bf16[1,128,2048]{2,1,0:T(8,128)(2,1)S(1)}, bf16[1,128,2048]{2,1,0:T(8,128)(2,1)}, u32[]{:S(2)}) copy-start(bf16[1,128,2048]{2,1,0:T(8,128)(2,1)} %param.12) | copy-start | bytes 1572868
  149.8 2.6 %copy-start.2 = (bf16[1,128,2048]{2,1,0:T(8,128)(2,1)S(1)}, bf16[1,128,2048]{2,1,0:T(8,128)(2,1)}, u32[]{:S(2)}) copy-start(bf16[1,128,2048]{2,1,0:T(8,128)(2,1)} %param.13) | copy-start | bytes 1572868
  149.8 2.6 %copy-start.3 = (bf16[1,128,2048]{2,1,0:T(8,128)(2,1)S(1)}, bf16[1,128,2048]{2,1,0:T(8,128)(2,1)}, u32[]{:S(2)}) copy-start(bf16[1,128,2048]{2,1,0:T(8,128)(2,1)} %param.14) | copy-start | bytes 1572868
  149.8 2.6 %copy-start.4 = (f32[2048]{0:T(1024)S(1)}, f32[2048]{0:T(1024)}, u32[]{:S(2)}) copy-start(f32[2048]{0:T(1024)} %param.16) | copy-start | bytes 24580
  149.9 4.5 %collective-permute-start = (f32[128,256]{1,0:T(8,128)S(1)}, f32[128,256]{1,0:T(8,128)S(1)}, u32[]{:S(2)}, u32[]{:S(2)}) collective-permute-start(f32[128,256]{1,0:T(8,128)S(1)} %get-tuple-element.13.refs_0_), channel_id=1, source_target_pairs={{0,2},{1,3},{2,0},{3,1},{4,6},{5,7},{6,4},{7,5},{8,10},{9,11},{10,... | collective-permute-start | bytes 393224 | tf_op jit(solution)/shard_map/ppermute | solution.py:310
  150.1 6.9 %collective-permute-start.2 = (f32[128,256]{1,0:T(8,128)S(1)}, f32[128,256]{1,0:T(8,128)S(1)}, u32[]{:S(2)}, u32[]{:S(2)}) collective-permute-start(f32[128,256]{1,0:T(8,128)S(1)} %get-tuple-element.13.refs_0_), channel_id=1, source_target_pairs={{0,1},{1,0},{2,3},{3,2},{4,5},{5,4},{6,7},{7,6},{8,9},{9,8},{10,11... | collective-permute-start | bytes 393224 | tf_op jit(solution)/shard_map/ppermute | solution.py:311
  151.6 5.4 %collective-permute-start.3 = (f32[128,256]{1,0:T(8,128)S(1)}, f32[128,256]{1,0:T(8,128)S(1)}, u32[]{:S(2)}, u32[]{:S(2)}) collective-permute-start(f32[128,256]{1,0:T(8,128)S(1)} %get-tuple-element.18.refs_1_), channel_id=1, source_target_pairs={{0,1},{1,0},{2,3},{3,2},{4,5},{5,4},{6,7},{7,6},{8,9},{9,8},{10,11... | collective-permute-start | bytes 393224 | tf_op jit(solution)/shard_map/ppermute | solution.py:311
  151.6 6.3 %collective-permute-start.1 = (f32[128,256]{1,0:T(8,128)S(1)}, f32[128,256]{1,0:T(8,128)S(1)}, u32[]{:S(2)}, u32[]{:S(2)}) collective-permute-start(f32[128,256]{1,0:T(8,128)S(1)} %get-tuple-element.18.refs_1_), channel_id=1, source_target_pairs={{0,2},{1,3},{2,0},{3,1},{4,6},{5,7},{6,4},{7,5},{8,10},{9,11},{10,... | collective-permute-start | bytes 393224 | tf_op jit(solution)/shard_map/ppermute | solution.py:310
  154.4 4.3 %collective-permute-start.4 = (f32[128,256]{1,0:T(8,128)S(1)}, f32[128,256]{1,0:T(8,128)S(1)}, u32[]{:S(2)}, u32[]{:S(2)}) collective-permute-start(f32[128,256]{1,0:T(8,128)S(1)} %collective-permute-done.refs_4_), channel_id=1, source_target_pairs={{0,1},{1,0},{2,3},{3,2},{4,5},{5,4},{6,7},{7,6},{8,9},{9,8},{10,11... | collective-permute-start | bytes 393224 | tf_op jit(solution)/shard_map/ppermute | solution.py:320
  157.9 1.8 %collective-permute-start.5 = (f32[128,256]{1,0:T(8,128)S(1)}, f32[128,256]{1,0:T(8,128)S(1)}, u32[]{:S(2)}, u32[]{:S(2)}) collective-permute-start(f32[128,256]{1,0:T(8,128)S(1)} %collective-permute-done.1.refs_2_), channel_id=1, source_target_pairs={{0,1},{1,0},{2,3},{3,2},{4,5},{5,4},{6,7},{7,6},{8,9},{9,8},{10,11... | collective-permute-start | bytes 393224 | tf_op jit(solution)/shard_map/ppermute | solution.py:325

commit v4 on v3

--- a/solution.py
+++ b/solution.py
@@ -271,7 +271,7 @@
     gates = (query_gate[0], key_gate[0], value_in[0], grad_out[0])
     pieces = jax.ShapeDtypeStruct((devices * piece, rows), f32)
     size = devices * piece * rows * 4
-    parts = 4
+    parts = 2
     sent = pl.pallas_call(
         functools.partial(pack_kernel, slots, parts),
         out_shape=pieces,

time: 161 us -> 161 us (level)
  no operation moved by 1% of the time
where the time goes in v4:
time: 161 us; the launch traced here: 160 us
  blocking collectives  140 us (87%)
  Pallas kernels  12.9 us (8%)
  starting transfers between devices  5.9 us (4%)
    all_to_all x2, blocking collectives, exchange(): lax.all_to_all(flat, ('seq', 'grp'), split_axis=0, concat_axis=0, tiled=T...  140 us
    pallas_call x1, Pallas kernels, body(): local_call(functools.partial(spectral_kernel, slots, groups, blocks), pie...  7.11 us
  transfers between devices with their start and end apart: 6, of which 2 were waited for; matrix products, arithmetic and copies ran while one was open for 0% of the time, Pallas kernels for 2%

profile of v4, /device:TPU:1, one launch (start us, length us, event | category | flops | bytes accessed | tf_op | source)
XLA Modules:
  0.0 160.3 jit_solution(14831307337962340775)
XLA Ops:
  0.6 2.1 %shard_map.138 = f32[4608,128]{1,0:T(8,128)S(1)} custom-call(s32[1]{0:T(128)} %bitcast.grp_ref, bf16[128,2048]{1,0:T(8,128)(2,1)} %bitcast.18, bf16[128,2048]{1,0:T(8,128)(2,1)} %bitcast.20, bf16[128,2048]{1,0:T(8,128)(2,1)} %bitcast.22, bf16[128,2048]{1,0:T(8,128)(2,1)} %bitcast.24, f32[128,2048]{1,0:T(8,128)} %refs_4_.1), custom_call_target="tpu_custom_call" | custom-call | bytes 4718592 | tf_op jit(solution)/shard_map/pallas_call | solution.py:275
  2.8 0.0 copy-start.5
  2.8 0.0 copy-start.6
  2.8 0.0 copy-start.7
  2.8 0.0 copy-start.8
  2.8 0.0 copy-start.9
  2.8 74.6 %all_to_all.10 = f32[256,1,2304]{2,1,0:T(1,128)S(1)} all-to-all(f32[256,1,2304]{2,1,0:T(1,128)S(1)} %bitcast.15), channel_id=1, replica_groups=mesh['seq'=64,'grp'=4] {'seq','grp'}, dimensions={0} | all-to-all | bytes 4718592 | tf_op jit(solution)/shard_map/all_to_all | solution.py:258
  77.5 7.1 %shard_map.139 = f32[4608,128]{1,0:T(8,128)S(1)} custom-call(f32[4608,128]{1,0:T(8,128)S(1)} %bitcast.16, bf16[128,192]{1,0:T(8,128)(2,1)S(1)} %copy-done.8, f32[2,64,128]{2,1,0:T(8,128)S(1)} %copy-done.7, bf16[768,256]{1,0:T(8,128)(2,1)S(1)} %copy-done.6, bf16[768,256]{1,0:T(8,128)(2,1)S(1)} %copy-done.5, bf16[64,384]{1,0:T(8,128)(2,1)S(1)} %copy-done.9), custom_call_target="tpu_custom_call" | custom-call | flops 5000000000 | bytes 4718592 | tf_op jit(solution)/shard_map/pallas_call | solution.py:298
  84.6 65.0 %all_to_all.11 = f32[256,1,2304]{2,1,0:T(1,128)S(1)} all-to-all(f32[256,1,2304]{2,1,0:T(1,128)S(1)} %bitcast.17), channel_id=1, replica_groups=mesh['seq'=64,'grp'=4] {'seq','grp'}, dimensions={0} | all-to-all | bytes 4718592 | tf_op jit(solution)/shard_map/all_to_all | solution.py:258
  149.6 0.0 copy-start.4
  149.6 0.1 shard_map.140
  149.8 0.2 collective-permute-start
  150.0 1.5 collective-permute-start.2
  151.5 0.0 collective-permute-start.3
  151.5 0.8 collective-permute-start.1
  152.3 1.9 %shard_map.141 = (bf16[128,2048]{1,0:T(8,128)(2,1)}, bf16[128,2048]{1,0:T(8,128)(2,1)}, bf16[128,2048]{1,0:T(8,128)(2,1)}) custom-call(bf16[128,2048]{1,0:T(8,128)(2,1)S(1)} %bitcast.19, bf16[128,2048]{1,0:T(8,128)(2,1)S(1)} %bitcast.21, bf16[128,2048]{1,0:T(8,128)(2,1)S(1)} %bitcast.23, bf16[128,2048]{1,0:T(8,128)(2,1)S(1)} %bitcast.25, ...), custom_call_target="tpu_custom_call" | custom-call | bytes 47185920 | tf_op jit(solution)/shard_map/pallas_call | solution.py:313
  154.2 0.1 collective-permute-done.refs_4_
  154.3 2.6 %collective-permute-start.4 = (f32[128,256]{1,0:T(8,128)S(1)}, f32[128,256]{1,0:T(8,128)S(1)}, u32[]{:S(2)}, u32[]{:S(2)}) collective-permute-start(f32[128,256]{1,0:T(8,128)S(1)} %collective-permute-done.refs_4_), channel_id=1, source_target_pairs={{0,1},{1,0},{2,3},{3,2},{4,5},{5,4},{6,7},{7,6},{8,9},{9,8},{10,11... | collective-permute-start | bytes 393224 | tf_op jit(solution)/shard_map/ppermute | solution.py:320
  156.9 0.0 collective-permute-done.2.refs_2_
  156.9 0.9 shard_map.142.refs_0_
  157.8 0.8 collective-permute-start.5
  158.6 0.0 collective-permute-done.4.refs_1_
  158.6 1.0 collective-permute-done.5.refs_3_
  159.6 0.8 shard_map.143
  (16 shorter events, 0.0 us)
Async XLA Ops:
  2.8 74.7 %copy-start.5 = (bf16[768,256]{1,0:T(8,128)(2,1)S(1)}, bf16[768,256]{1,0:T(8,128)(2,1)}, u32[]{:S(2)}) copy-start(bf16[768,256]{1,0:T(8,128)(2,1)} %constant.17.clone.back_ref) | copy-start | bytes 1179652
  2.8 74.7 %copy-start.6 = (bf16[768,256]{1,0:T(8,128)(2,1)S(1)}, bf16[768,256]{1,0:T(8,128)(2,1)}, u32[]{:S(2)}) copy-start(bf16[768,256]{1,0:T(8,128)(2,1)} %constant.16.clone.ahead_ref) | copy-start | bytes 1179652
  2.8 74.7 %copy-start.7 = (f32[2,64,128]{2,1,0:T(8,128)S(1)}, f32[2,64,128]{2,1,0:T(8,128)}, u32[]{:S(2)}) copy-start(f32[2,64,128]{2,1,0:T(8,128)} %constant.15.clone.turn_ref) | copy-start | bytes 196612
  2.8 74.7 %copy-start.8 = (bf16[128,192]{1,0:T(8,128)(2,1)S(1)}, bf16[128,192]{1,0:T(8,128)(2,1)}, u32[]{:S(2)}) copy-start(bf16[128,192]{1,0:T(8,128)(2,1)} %constant.14.clone.first_ref) | copy-start | bytes 147460
  2.8 74.7 %copy-start.9 = (bf16[64,384]{1,0:T(8,128)(2,1)S(1)}, bf16[64,384]{1,0:T(8,128)(2,1)}, u32[]{:S(2)}) copy-start(bf16[64,384]{1,0:T(8,128)(2,1)} %constant.18.clone.last_ref) | copy-start | bytes 147460
  149.6 2.6 %copy-start = (bf16[1,128,2048]{2,1,0:T(8,128)(2,1)S(1)}, bf16[1,128,2048]{2,1,0:T(8,128)(2,1)}, u32[]{:S(2)}) copy-start(bf16[1,128,2048]{2,1,0:T(8,128)(2,1)} %param.11) | copy-start | bytes 1572868
  149.6 2.6 %copy-start.1 = (bf16[1,128,2048]{2,1,0:T(8,128)(2,1)S(1)}, bf16[1,128,2048]{2,1,0:T(8,128)(2,1)}, u32[]{:S(2)}) copy-start(bf16[1,128,2048]{2,1,0:T(8,128)(2,1)} %param.12) | copy-start | bytes 1572868
  149.6 2.6 %copy-start.2 = (bf16[1,128,2048]{2,1,0:T(8,128)(2,1)S(1)}, bf16[1,128,2048]{2,1,0:T(8,128)(2,1)}, u32[]{:S(2)}) copy-start(bf16[1,128,2048]{2,1,0:T(8,128)(2,1)} %param.13) | copy-start | bytes 1572868
  149.6 2.6 %copy-start.3 = (bf16[1,128,2048]{2,1,0:T(8,128)(2,1)S(1)}, bf16[1,128,2048]{2,1,0:T(8,128)(2,1)}, u32[]{:S(2)}) copy-start(bf16[1,128,2048]{2,1,0:T(8,128)(2,1)} %param.14) | copy-start | bytes 1572868
  149.6 2.6 %copy-start.4 = (f32[2048]{0:T(1024)S(1)}, f32[2048]{0:T(1024)}, u32[]{:S(2)}) copy-start(f32[2048]{0:T(1024)} %param.16) | copy-start | bytes 24580
  149.8 4.5 %collective-permute-start = (f32[128,256]{1,0:T(8,128)S(1)}, f32[128,256]{1,0:T(8,128)S(1)}, u32[]{:S(2)}, u32[]{:S(2)}) collective-permute-start(f32[128,256]{1,0:T(8,128)S(1)} %get-tuple-element.13.refs_0_), channel_id=1, source_target_pairs={{0,2},{1,3},{2,0},{3,1},{4,6},{5,7},{6,4},{7,5},{8,10},{9,11},{10,... | collective-permute-start | bytes 393224 | tf_op jit(solution)/shard_map/ppermute | solution.py:310
  150.0 6.9 %collective-permute-start.2 = (f32[128,256]{1,0:T(8,128)S(1)}, f32[128,256]{1,0:T(8,128)S(1)}, u32[]{:S(2)}, u32[]{:S(2)}) collective-permute-start(f32[128,256]{1,0:T(8,128)S(1)} %get-tuple-element.13.refs_0_), channel_id=1, source_target_pairs={{0,1},{1,0},{2,3},{3,2},{4,5},{5,4},{6,7},{7,6},{8,9},{9,8},{10,11... | collective-permute-start | bytes 393224 | tf_op jit(solution)/shard_map/ppermute | solution.py:311
  151.5 5.4 %collective-permute-start.3 = (f32[128,256]{1,0:T(8,128)S(1)}, f32[128,256]{1,0:T(8,128)S(1)}, u32[]{:S(2)}, u32[]{:S(2)}) collective-permute-start(f32[128,256]{1,0:T(8,128)S(1)} %get-tuple-element.18.refs_1_), channel_id=1, source_target_pairs={{0,1},{1,0},{2,3},{3,2},{4,5},{5,4},{6,7},{7,6},{8,9},{9,8},{10,11... | collective-permute-start | bytes 393224 | tf_op jit(solution)/shard_map/ppermute | solution.py:311
  151.5 6.3 %collective-permute-start.1 = (f32[128,256]{1,0:T(8,128)S(1)}, f32[128,256]{1,0:T(8,128)S(1)}, u32[]{:S(2)}, u32[]{:S(2)}) collective-permute-start(f32[128,256]{1,0:T(8,128)S(1)} %get-tuple-element.18.refs_1_), channel_id=1, source_target_pairs={{0,2},{1,3},{2,0},{3,1},{4,6},{5,7},{6,4},{7,5},{8,10},{9,11},{10,... | collective-permute-start | bytes 393224 | tf_op jit(solution)/shard_map/ppermute | solution.py:310
  154.3 4.3 %collective-permute-start.4 = (f32[128,256]{1,0:T(8,128)S(1)}, f32[128,256]{1,0:T(8,128)S(1)}, u32[]{:S(2)}, u32[]{:S(2)}) collective-permute-start(f32[128,256]{1,0:T(8,128)S(1)} %collective-permute-done.refs_4_), channel_id=1, source_target_pairs={{0,1},{1,0},{2,3},{3,2},{4,5},{5,4},{6,7},{7,6},{8,9},{9,8},{10,11... | collective-permute-start | bytes 393224 | tf_op jit(solution)/shard_map/ppermute | solution.py:320
  157.8 1.8 %collective-permute-start.5 = (f32[128,256]{1,0:T(8,128)S(1)}, f32[128,256]{1,0:T(8,128)S(1)}, u32[]{:S(2)}, u32[]{:S(2)}) collective-permute-start(f32[128,256]{1,0:T(8,128)S(1)} %collective-permute-done.1.refs_2_), channel_id=1, source_target_pairs={{0,1},{1,0},{2,3},{3,2},{4,5},{5,4},{6,7},{7,6},{8,9},{9,8},{10,11... | collective-permute-start | bytes 393224 | tf_op jit(solution)/shard_map/ppermute | solution.py:325
